TPU v7x, 128 devices: a whole 4x4x4 slice. The times are simulated.
128 devices in a mesh: ops: 32 (over x, z, core), sec: 4 (over y).
Axes of the slice: x: 4, y: 4, z: 4, core: 2. Of those that a mesh axis runs over, the one named last changes fastest.
Arguments:
- wave_in: bfloat16 [4096, 4096], P('sec', 'ops'), may hold values from -16 to 16
- row_energy: float32 [4096], P('sec'), may hold values from 1 to 4
- row_operators: bfloat16 [128, 4096, 512], P('ops', 'sec'), may hold values from -0.25 to 0.25
- column_operators: bfloat16 [128, 512, 512], P('ops'), may hold values from -0.52734375 to 0.52734375
- term_count: int32 [32], P('ops'), may hold values from 1 to 4, 48 in all
- source: int32 [128], P('ops'), may hold values from 0 to 7
- target: int32 [128], P('ops'), may hold values from 0 to 7
Outputs:
- wave_next: float32 [4096, 4096], P('sec', 'ops')
- renormalized: float32 [128, 4096, 512], P('ops', 'sec')
- energy: float32 [], replicated
Inputs may be any that keep to these rules, and one draw needn't show every extreme that they name: `term_count`: the counts sum to 48, and some index of ops holds exactly 4 terms.
All inputs are finite; a program needn't handle non-finite values. No bound on the sum of `term_count` on one device may be relied on, other than what follows from the above.
Results may differ from a plain program's by a relative error of at most 0.0095.
Values may be sent and summed in bfloat16 or wider, within the bound.
A program may use at most 128 MiB of HBM per device.

v0:
```python
import functools

import jax
import jax.numpy as jnp
from jax import lax
from jax.experimental import pallas as pl
from jax.experimental.pallas import tpu as pltpu
from jax.sharding import Mesh
from jax.sharding import PartitionSpec as P

SEC = 512
COLS = 4096
ENTRIES = 4096 * 4096
CHIPS = 16
WIDE = 256
HALF = 256
QUARTER = 128
MIB = 1 << 20
MESH = pl.DeviceIdType.MESH
OPS = ("x", "z", "core")
F32 = jnp.float32
BF16 = jnp.bfloat16


def turn(place, by):
    return lax.rem(place + (by + 4), 4)


def push(src, dst, send, recv, to):
    return pltpu.make_async_remote_copy(
        src_ref=src, dst_ref=dst, send_sem=send, recv_sem=recv, device_id=to, device_id_type=MESH
    )


def greet(peers):
    barrier = pltpu.get_barrier_semaphore()
    for peer in peers:
        pl.semaphore_signal(barrier, inc=1, device_id=peer, device_id_type=MESH)
    pl.semaphore_wait(barrier, len(peers))


def all_blocks(buf, x, z, send, recv):
    names = (("x", "z"), ("z", "x"))
    places = ((x, z), (z, x))

    def block(h, pa, pb):
        return pa * 4 + pb if h == 0 else pb * 4 + pa

    def view(h, pa, pb, part):
        rows = pl.ds(h * HALF, HALF) if part is None else pl.ds(h * HALF + part * QUARTER, QUARTER)
        return buf.at[block(h, pa, pb), rows, :]

    def copy(h, j, pa, pb, part, axis, by):
        ref = view(h, pa, pb, part)
        to = {names[h][axis]: turn(places[h][axis], by)}
        return push(ref, ref, send.at[h, j], recv.at[h, j], to)

    def order(h):
        p = places[h][0]
        return (p, turn(p, -1), turn(p, 1), turn(p, 2))

    sent = []

    def go(*what):
        one = copy(*what)
        one.start()
        sent.append(one)

    def arrived(h, j, pa, pb, part):
        copy(h, j, pa, pb, part, 0, 1).wait_recv()

    for h in (0, 1):
        p, q = places[h]
        go(h, 0, p, q, None, 0, 1)
        go(h, 1, p, q, None, 0, -1)
    for h in (0, 1):
        p, q = places[h]
        go(h, 4, p, q, None, 1, 1)
        go(h, 8, p, q, None, 1, -1)
    yield
    for h in (0, 1):
        p, q = places[h]
        left, right = turn(p, -1), turn(p, 1)
        arrived(h, 0, left, q, None)
        go(h, 2, left, q, 0, 0, 1)
        go(h, 5, left, q, None, 1, 1)
        go(h, 9, left, q, None, 1, -1)
        arrived(h, 1, right, q, None)
        go(h, 3, right, q, 1, 0, -1)
        go(h, 6, right, q, None, 1, 1)
        go(h, 10, right, q, None, 1, -1)
    yield

    def onward(h, i):
        pa, q = order(h)[i], places[h][1]
        arrived(h, 4 + i, pa, turn(q, -1), None)
        go(h, 12 + i, pa, turn(q, -1), 0, 1, 1)
        arrived(h, 8 + i, pa, turn(q, 1), None)
        go(h, 16 + i, pa, turn(q, 1), 1, 1, -1)

    for h in (0, 1):
        onward(h, 0)
    yield
    for h in (0, 1):
        p, q = places[h]
        far = turn(p, 2)
        arrived(h, 2, far, q, 0)
        arrived(h, 3, far, q, 1)
        go(h, 7, far, q, None, 1, 1)
        go(h, 11, far, q, None, 1, -1)
    yield
    for i in (1, 2, 3):
        for h in (0, 1):
            onward(h, i)
        yield
    for i in range(4):
        for h in (0, 1):
            pa, far = order(h)[i], turn(places[h][1], 2)
            arrived(h, 12 + i, pa, far, 0)
            arrived(h, 16 + i, pa, far, 1)
    for one in sent:
        one.wait_send()


def ring_peers(x, z):
    return [{"x": turn(x, 1)}, {"x": turn(x, -1)}, {"z": turn(z, 1)}, {"z": turn(z, -1)}]


def gather_kernel(
    wave, row_ops, col_ops, table, wide, row_sib, col_sib, table_sib, send, recv, swap_send, swap_recv, own_sem
):
    x, z, c = lax.axis_index("x"), lax.axis_index("z"), lax.axis_index("core")
    sib = {"core": 1 - c}
    greet(ring_peers(x, z) + [sib])
    b = x * 4 + z
    mine = pl.ds(pl.multiple_of(c * SEC, SEC), SEC)
    other = pl.ds(pl.multiple_of((1 - c) * SEC, SEC), SEC)
    columns = pl.ds(pl.multiple_of(c * 128, 128), 128)
    other_columns = pl.ds(pl.multiple_of((1 - c) * 128, 128), 128)
    own = pltpu.make_async_copy(wave.at[mine, :], wide.at[b, :, columns], own_sem)
    swaps = [
        push(wave.at[other, :], wide.at[b, :, columns], swap_send.at[0], swap_recv.at[0], sib),
        push(table, table_sib, swap_send.at[1], swap_recv.at[1], sib),
        push(row_ops.at[:, other, :], row_sib, swap_send.at[2], swap_recv.at[2], sib),
        push(col_ops, col_sib, swap_send.at[3], swap_recv.at[3], sib),
    ]
    swaps[0].start()
    own.start()
    own.wait()
    push(wave.at[other, :], wide.at[b, :, other_columns], swap_send.at[0], swap_recv.at[0], sib).wait_recv()
    steps = all_blocks(wide, x, z, send, recv)
    next(steps)
    for swap in swaps[1:]:
        swap.start()
    for step in steps:
        del step
    swaps[0].wait_send()
    for swap in swaps[1:]:
        swap.wait()


def gather(wave, row_ops, col_ops, table):
    hbm = pl.BlockSpec(memory_space=pl.ANY)
    return pl.pallas_call(
        gather_kernel,
        out_shape=(
            jax.ShapeDtypeStruct((CHIPS, SEC, WIDE), BF16),
            jax.ShapeDtypeStruct((4, SEC, SEC), BF16),
            jax.ShapeDtypeStruct((4, SEC, SEC), BF16),
            jax.ShapeDtypeStruct((8, 128), jnp.int32),
        ),
        in_specs=[hbm] * 4,
        out_specs=(hbm,) * 4,
        scratch_shapes=[
            pltpu.SemaphoreType.DMA((2, 20)),
            pltpu.SemaphoreType.DMA((2, 20)),
            pltpu.SemaphoreType.DMA((4,)),
            pltpu.SemaphoreType.DMA((4,)),
            pltpu.SemaphoreType.DMA(()),
        ],
        compiler_params=pltpu.CompilerParams(collective_id=0, has_side_effects=True),
        name="gather",
    )(wave, row_ops, col_ops, table)


def dot(a, b):
    return jnp.dot(a, b, preferred_element_type=F32)


def dot_t(a, b):
    return lax.dot_general(a, b, (((1,), (1,)), ((), ())), preferred_element_type=F32)


def terms_kernel(
    table, table_sib, row_ops, row_sib, col_ops, col_sib, wide, out, wide_v, row_v, col_v, total, wide_sem, row_sem, col_sem
):
    c = table[0, 9]
    mine = pl.ds(pl.multiple_of(c * SEC, SEC), SEC)
    counts = (table[0, 0], table_sib[0, 0])
    load = pltpu.make_async_copy(wide, wide_v, wide_sem)
    load.start()

    def copies(side, k):
        slot = side * 4 + k
        rows = (row_ops.at[k, mine, :], row_sib.at[k])[side]
        cols = (col_ops.at[k], col_sib.at[k])[side]
        return (
            pltpu.make_async_copy(rows, row_v.at[slot], row_sem.at[slot]),
            pltpu.make_async_copy(cols, col_v.at[slot], col_sem.at[slot]),
        )

    for k in range(4):
        for side in (0, 1):

            @pl.when(k < counts[side])
            def start(side=side, k=k):
                for one in copies(side, k):
                    one.start()

    def clear(i, carry):
        total[i] = jnp.zeros((SEC, WIDE), F32)
        return carry

    lax.fori_loop(0, CHIPS, clear, 0)
    load.wait()
    for side in (0, 1):
        this = (table, table_sib)[side]

        def term(k, carry, side=side, this=this):
            slot = side * 4 + k
            src = this[0, 1 + k] * 2
            tgt = this[0, 5 + k] * 2
            for one in copies(side, k):
                one.wait()
            rows = row_v[slot]
            first = dot(rows, wide_v[src]).astype(BF16)
            second = dot(rows, wide_v[src + 1]).astype(BF16)
            for part in (0, 1):
                where = pl.ds(part * WIDE, WIDE)
                total[tgt + part] += dot(first, col_v[slot, :WIDE, where]) + dot(second, col_v[slot, WIDE:, where])
            return carry

        lax.fori_loop(0, counts[side], term, 0)

    def finish(i, carry):
        out[i] = total[i].astype(BF16)
        return carry

    lax.fori_loop(0, CHIPS, finish, 0)


def terms(table, table_sib, row_ops, row_sib, col_ops, col_sib, wide):
    hbm = pl.BlockSpec(memory_space=pl.ANY)
    smem = pl.BlockSpec(memory_space=pltpu.SMEM)
    return pl.pallas_call(
        terms_kernel,
        out_shape=jax.ShapeDtypeStruct((CHIPS, SEC, WIDE), BF16),
        in_specs=[smem, smem] + [hbm] * 5,
        out_specs=pl.BlockSpec(memory_space=pltpu.VMEM),
        scratch_shapes=[
            pltpu.VMEM((CHIPS, SEC, WIDE), BF16),
            pltpu.VMEM((8, SEC, SEC), BF16),
            pltpu.VMEM((8, SEC, SEC), BF16),
            pltpu.VMEM((CHIPS, SEC, WIDE), F32),
            pltpu.SemaphoreType.DMA(()),
            pltpu.SemaphoreType.DMA((8,)),
            pltpu.SemaphoreType.DMA((8,)),
        ],
        compiler_params=pltpu.CompilerParams(vmem_limit_bytes=48 * MIB),
        name="terms",
    )(table, table_sib, row_ops, row_sib, col_ops, col_sib, wide)


def rough(a, b):
    return dot(a.astype(BF16), b.astype(BF16))


def reduce_blocks(part, near, whole, near2, whole2, total, x, z, send, recv, send2, recv2):
    names = (("z", "x"), ("x", "z"))
    places = ((z, x), (x, z))

    def block(h, pa, pb):
        return pb * 4 + pa if h == 0 else pa * 4 + pb

    def rows(h, half):
        return pl.ds(h * HALF + half * QUARTER, QUARTER)

    def local(half):
        return pl.ds(half * QUARTER, QUARTER)

    def order(h):
        q = places[h][1]
        return (turn(q, 2), turn(q, 1), turn(q, -1), q)

    sent = []

    def go(one):
        one.start()
        sent.append(one)

    def near_copy(h, d, i):
        p = places[h][0]
        src = part.at[block(h, turn(p, 2), order(h)[i]), rows(h, d), :]
        to = {names[h][0]: turn(p, 1 - 2 * d)}
        return push(src, near.at[h, d, i], send.at[h, d, i], recv.at[h, d, i], to)

    def whole_copy(h, d, i, half):
        p = places[h][0]
        src = part.at[block(h, turn(p, 1 - 2 * d), order(h)[i]), rows(h, half), :]
        to = {names[h][0]: turn(p, 1 - 2 * d)}
        j = 2 + 2 * d + half
        return push(src, whole.at[h, d, i, local(half), :], send.at[h, j, i], recv.at[h, j, i], to)

    def near2_copy(h, d):
        p, q = places[h]
        src = part.at[block(h, p, turn(q, 2)), rows(h, d), :]
        return push(src, near2.at[h, d], send2.at[h, d], recv2.at[h, d], {names[h][1]: turn(q, 1 - 2 * d)})

    def whole2_copy(h, d, half):
        p, q = places[h]
        j = 2 + 2 * d + half
        src = part.at[block(h, p, turn(q, 1 - 2 * d)), rows(h, half), :]
        to = {names[h][1]: turn(q, 1 - 2 * d)}
        return push(src, whole2.at[h, d, local(half), :], send2.at[h, j], recv2.at[h, j], to)

    for i in range(4):
        for h in (0, 1):
            for d in (0, 1):
                go(near_copy(h, d, i))
    for i in range(4):
        for h in (0, 1):
            for d in (0, 1):
                go(whole_copy(h, d, i, 1 - d))
    for i in range(4):
        for h in (0, 1):
            p = places[h][0]
            for d in (0, 1):
                near_copy(h, d, i).wait_recv()
                at = block(h, turn(p, 1 - 2 * d), order(h)[i])
                both = part[at, rows(h, d), :].astype(F32) + near[h, d, i].astype(F32)
                part[at, rows(h, d), :] = both.astype(BF16)
                go(whole_copy(h, d, i, d))
    for i in range(4):
        for h in (0, 1):
            p, q = places[h]
            for d in (0, 1):
                for half in (0, 1):
                    whole_copy(h, d, i, half).wait_recv()
            at = block(h, p, order(h)[i])
            here = pl.ds(h * HALF, HALF)
            done = part[at, here, :].astype(F32) + whole[h, 0, i].astype(F32) + whole[h, 1, i].astype(F32)
            if i == 3:
                total[here, :] = done
            else:
                part[at, here, :] = done.astype(BF16)
            if i == 0:
                go(near2_copy(h, 0))
                go(near2_copy(h, 1))
            if i == 1:
                go(whole2_copy(h, 0, 1))
            if i == 2:
                go(whole2_copy(h, 1, 0))
    for h in (0, 1):
        p, q = places[h]
        for d in (0, 1):
            near2_copy(h, d).wait_recv()
            at = block(h, p, turn(q, 1 - 2 * d))
            both = part[at, rows(h, d), :].astype(F32) + near2[h, d].astype(F32)
            part[at, rows(h, d), :] = both.astype(BF16)
            go(whole2_copy(h, d, d))
    for h in (0, 1):
        for d in (0, 1):
            for half in (0, 1):
                whole2_copy(h, d, half).wait_recv()
        here = pl.ds(h * HALF, HALF)
        total[here, :] += whole2[h, 0].astype(F32) + whole2[h, 1].astype(F32)
    for one in sent:
        one.wait_send()


def frobenius(a):
    return jnp.sqrt(jnp.sum(a * a, axis=(0, 1), keepdims=True) + 1e-06)


def step_kernel(
    part_h, wide_h, energy_col,
    stepped_o, root_o, level_o, exact_o, energy_o,
    part, near, whole, near2, whole2, total, wide, summed, stepped, gram, my, mm, mu, mz, roots, level_two, exact, scalars,
    rs_send, rs_recv, rs2_send, rs2_recv, ag_send, ag_recv, en_send, en_recv, st_send, st_recv, st_own,
    end_send, end_recv, own_sem,
):
    x, z, c, y = lax.axis_index("x"), lax.axis_index("z"), lax.axis_index("core"), lax.axis_index("sec")
    b = x * 4 + z
    sib = {"core": 1 - c}
    load = pltpu.make_async_copy(part_h, part, own_sem.at[0])
    load_wide = pltpu.make_async_copy(wide_h, wide, own_sem.at[1])
    load.start()
    greet(
        ring_peers(x, z)
        + [{"x": turn(x, 2)}, {"z": turn(z, 2)}, sib, {"sec": turn(y, 1)}, {"sec": turn(y, 2)}, {"sec": turn(y, -1)}]
    )
    load.wait()
    load_wide.start()
    reduce_blocks(part, near, whole, near2, whole2, total, x, z, rs_send, rs_recv, rs2_send, rs2_recv)
    summed[b] = total[...].astype(BF16)
    steps = all_blocks(summed, x, z, ag_send, ag_recv)
    next(steps)
    load_wide.wait()
    level = energy_col[pl.ds(pl.multiple_of(c * SEC, SEC), SEC), :]
    amplitude = wide[b].astype(F32)
    applied = level * amplitude + total[...]
    share = jnp.sum(amplitude * applied, axis=(0, 1), keepdims=True)

    stages = (("sec", y, 4), ("x", x, 4), ("z", z, 4), ("core", c, 2))

    def energy_copies(s):
        name, place, size = stages[s]
        for hop in range(1, size):
            to = {name: lax.rem(place + hop, size)}
            src = lax.rem(place + (size - hop), size)
            yield (
                push(scalars.at[s, place], scalars.at[s, place], en_send.at[s, hop], en_recv.at[s, hop], to),
                push(scalars.at[s, src], scalars.at[s, src], en_send.at[s, hop], en_recv.at[s, hop], to),
            )

    for s in range(4):
        place, size = stages[s][1:]
        scalars[s, place] = jnp.broadcast_to(share, (8, 128))
        for out, unused in energy_copies(s):
            out.start()
        next(steps, None)
        for out, arriving in energy_copies(s):
            arriving.wait_recv()
            out.wait_send()
        share = scalars[s, 0] + scalars[s, 1]
        if size == 4:
            share = (share + scalars[s, 2]) + scalars[s, 3]
        share = share[0:1, 0:1]
    energy = share * (1.0 / ENTRIES)
    energy_o[...] = jnp.broadcast_to(energy, (8, 128))
    for step in steps:
        del step

    own = amplitude + 0.5 * (energy * amplitude - applied)
    exact[0] = own[:, :128]
    exact[1] = own[:, 128:]
    mine = pl.ds(pl.multiple_of(c * SEC, SEC), SEC)
    exact_send = push(exact.at[1 - c], exact_o.at[mine, :], end_send.at[0], end_recv.at[0], sib)
    exact_own = pltpu.make_async_copy(exact.at[c], exact_o.at[mine, :], own_sem.at[2])
    exact_send.start()
    exact_own.start()

    def out_block(i):
        return (
            push(stepped.at[i], stepped_o.at[c, i], st_send.at[i], st_recv.at[i], sib),
            pltpu.make_async_copy(stepped.at[i], stepped_o.at[c, i], st_own.at[i]),
        )

    gram[...] = jnp.zeros((SEC, SEC), F32)

    def one_block(i, carry):
        part_of = wide[i].astype(F32)
        value = part_of + 0.5 * (energy * part_of - (level * part_of + summed[i].astype(F32)))
        value = value.astype(BF16)
        stepped[i] = value
        for one in out_block(i):
            one.start()
        gram[...] += dot_t(value, value)
        return carry

    lax.fori_loop(0, CHIPS, one_block, 0)

    def root(y_ref, d_ref, again):
        my[...] = 1.5 * y_ref[...] - 0.5 * rough(y_ref[...], y_ref[...])
        mu[...] = 1.5 * my[...] - 0.5 * rough(y_ref[...], my[...])
        d_ref[...] = 0.25 * rough(mu[...], y_ref[...]) - 0.75 * (y_ref[...] + mu[...])
        if again:
            y_ref[...] = 1.5 * my[...] - 0.5 * rough(my[...], mu[...])

    gram_one = gram[...] * (1.0 / COLS)
    scale_one = frobenius(gram_one)
    gram[...] = gram_one / scale_one
    root(gram, mz, True)
    gram_two = 2.25 * gram[...] + rough(mz[...], gram[...])
    scale_two = frobenius(gram_two)
    gram[...] = gram_two / scale_two
    root(gram, mm, False)
    size = jnp.sqrt(scale_one) * jnp.sqrt(scale_two)
    roots[...] = ((2.25 * (mz[...] + mm[...]) + rough(mm[...], mz[...])) / size).astype(BF16)
    level_two[...] = jnp.broadcast_to(2.25 * 2.25 / size, (8, 128))
    root_send = push(roots, root_o.at[c], end_send.at[1], end_recv.at[1], sib)
    root_own = pltpu.make_async_copy(roots, root_o.at[c], own_sem.at[3])
    level_send = push(level_two, level_o.at[c], end_send.at[2], end_recv.at[2], sib)
    level_own = pltpu.make_async_copy(level_two, level_o.at[c], own_sem.at[4])
    level_send.start()
    level_own.start()
    root_send.start()
    root_own.start()

    def block_done(i, carry):
        going, staying = out_block(i)
        going.wait_send()
        staying.wait()
        push(stepped.at[i], stepped_o.at[1 - c, i], st_send.at[i], st_recv.at[i], sib).wait_recv()
        return carry

    lax.fori_loop(0, CHIPS, block_done, 0)
    other = pl.ds(pl.multiple_of((1 - c) * SEC, SEC), SEC)
    exact_send.wait_send()
    exact_own.wait()
    push(exact.at[1 - c], exact_o.at[other, :], end_send.at[0], end_recv.at[0], sib).wait_recv()
    root_send.wait_send()
    root_own.wait()
    push(roots, root_o.at[1 - c], end_send.at[1], end_recv.at[1], sib).wait_recv()
    level_send.wait_send()
    level_own.wait()
    push(level_two, level_o.at[1 - c], end_send.at[2], end_recv.at[2], sib).wait_recv()


def step(part, wide, energy_col):
    hbm = pl.BlockSpec(memory_space=pl.ANY)
    vmem = pl.BlockSpec(memory_space=pltpu.VMEM)
    square = pltpu.VMEM((SEC, SEC), F32)
    blocks = pltpu.VMEM((CHIPS, SEC, WIDE), BF16)
    dma = pltpu.SemaphoreType.DMA
    return pl.pallas_call(
        step_kernel,
        out_shape=(
            jax.ShapeDtypeStruct((2, CHIPS, SEC, WIDE), BF16),
            jax.ShapeDtypeStruct((2, SEC, SEC), BF16),
            jax.ShapeDtypeStruct((2, 8, 128), F32),
            jax.ShapeDtypeStruct((2 * SEC, 128), F32),
            jax.ShapeDtypeStruct((8, 128), F32),
        ),
        in_specs=[hbm, hbm, vmem],
        out_specs=(hbm, hbm, hbm, hbm, vmem),
        scratch_shapes=[
            blocks,
            pltpu.VMEM((2, 2, 4, QUARTER, WIDE), BF16),
            pltpu.VMEM((2, 2, 4, HALF, WIDE), BF16),
            pltpu.VMEM((2, 2, QUARTER, WIDE), BF16),
            pltpu.VMEM((2, 2, HALF, WIDE), BF16),
            pltpu.VMEM((SEC, WIDE), F32),
            blocks,
            blocks,
            blocks,
            square,
            square,
            square,
            square,
            square,
            pltpu.VMEM((SEC, SEC), BF16),
            pltpu.VMEM((8, 128), F32),
            pltpu.VMEM((2, SEC, 128), F32),
            pltpu.VMEM((4, 4, 8, 128), F32),
            dma((2, 6, 4)),
            dma((2, 6, 4)),
            dma((2, 6)),
            dma((2, 6)),
            dma((2, 20)),
            dma((2, 20)),
            dma((4, 4)),
            dma((4, 4)),
            dma((CHIPS,)),
            dma((CHIPS,)),
            dma((CHIPS,)),
            dma((3,)),
            dma((3,)),
            dma((5,)),
        ],
        compiler_params=pltpu.CompilerParams(
            collective_id=1, has_side_effects=True, vmem_limit_bytes=56 * MIB
        ),
        name="step",
    )(part, wide, energy_col)


def renorm_kernel(table, src_block, tgt_block, cols, root, level, exact, out, wave_o):
    k = pl.program_id(0)
    scale = level[0, 0:1, 0:1]

    @pl.when(k == 0)
    def first():
        wave_o[...] = scale * exact[...] + dot(root[0], exact[...].astype(BF16))

    @pl.when(k < table[0])
    def live():
        product = None
        for part in (0, 1):
            block = src_block[0, part]
            half = (scale * block.astype(F32) + dot(root[0], block)).astype(BF16)
            added = dot(half, cols[0, part * WIDE : (part + 1) * WIDE, :])
            product = added if product is None else product + added
        product = product.astype(BF16)
        total = None
        for part in (0, 1):
            block = tgt_block[0, part]
            half = (scale * block.astype(F32) + dot(root[0], block)).astype(BF16)
            added = dot_t(product[:, part * WIDE : (part + 1) * WIDE], half)
            total = added if total is None else total + added
        out[0] = total * SEC ** (-0.5)

    @pl.when(k >= table[0])
    def empty():
        out[...] = jnp.zeros_like(out)


def renorm(table, stepped, cols, root, level, exact):
    def slot(k, table):
        return jnp.minimum(k, table[0] - 1)

    def sector(k, s, table):
        return jnp.where(k < table[0], s, 1)

    def src_at(k, s, table):
        return (sector(k, s, table), table[1 + slot(k, table)], 0, 0)

    def tgt_at(k, s, table):
        return (sector(k, s, table), table[5 + slot(k, table)], 0, 0)

    return pl.pallas_call(
        renorm_kernel,
        out_shape=(
            jax.ShapeDtypeStruct((4, 2 * SEC, SEC), F32),
            jax.ShapeDtypeStruct((2 * SEC, 128), F32),
        ),
        grid_spec=pltpu.PrefetchScalarGridSpec(
            num_scalar_prefetch=1,
            grid=(4, 2),
            in_specs=[
                pl.BlockSpec((1, 2, SEC, WIDE), src_at),
                pl.BlockSpec((1, 2, SEC, WIDE), tgt_at),
                pl.BlockSpec((1, SEC, SEC), lambda k, s, table: (slot(k, table), 0, 0)),
                pl.BlockSpec((1, SEC, SEC), lambda k, s, table: (sector(k, s, table), 0, 0)),
                pl.BlockSpec((1, 8, 128), lambda k, s, table: (sector(k, s, table), 0, 0)),
                pl.BlockSpec((SEC, 128), lambda k, s, table: (jnp.where(k == 0, s, 1), 0)),
            ],
            out_specs=[
                pl.BlockSpec((1, SEC, SEC), lambda k, s, table: (k, s, 0)),
                pl.BlockSpec((SEC, 128), lambda k, s, table: (jnp.where(k == 0, s, 1), 0)),
            ],
        ),
        compiler_params=pltpu.CompilerParams(vmem_limit_bytes=32 * MIB),
        name="renorm",
    )(table, stepped, stepped, cols, root, level, exact)


def on_device(wave_in, row_energy, row_operators, column_operators, term_count, source, target):
    core = lax.axis_index("core").astype(jnp.int32).reshape(1)
    numbers = jnp.concatenate([term_count, source, target, core])
    table = jnp.pad(numbers.reshape(1, 10), ((0, 7), (0, 118)))
    wide, row_sib, col_sib, table_sib = gather(wave_in, row_operators, column_operators, table)
    part = terms(table, table_sib, row_operators, row_sib, column_operators, col_sib, wide)
    stepped, root, level, exact, energy = step(part, wide, row_energy.reshape(-1, 1))
    renormalized, wave_next = renorm(numbers, stepped, column_operators, root, level, exact)
    return (wave_next, renormalized, energy[0, 0])


def solution(mesh):
    torus = Mesh(mesh.devices.reshape(4, 4, 2, mesh.shape["sec"]), ("x", "z", "core", "sec"))
    return jax.shard_map(
        on_device,
        mesh=torus,
        in_specs=(
            P("sec", OPS),
            P("sec"),
            P(OPS, "sec", None),
            P(OPS, None, None),
            P(OPS),
            P(OPS),
            P(OPS),
        ),
        out_specs=(P("sec", OPS), P(OPS, "sec", None), P()),
        check_vma=False,
    )
```

profile of v0, /device:TPU:1, one launch (start us, length us, event | category | flops | bytes accessed | tf_op | source)
XLA Modules:
  0.0 138.4 jit_solution(2709103031570954552)
XLA Ops:
  0.6 0.0 copy-start.1
  1.4 0.8 pad_add_fusion.table
  2.2 0.6 pad.4.table
  2.8 0.0 copy-start.5
  2.8 1.7 %copy.10.energy_col = f32[1024,1]{1,0:T(8,128)} copy(f32[1024,1]{0,1:T(1,128)} %bitcast.5) | data formatting | bytes 8192 | tf_op jit(solution)/shard_map/reshape | solution.py:654
  4.5 34.5 %gather.1 = (bf16[16,512,256]{2,1,0:T(8,128)(2,1)}, bf16[4,512,512]{2,1,0:T(8,128)(2,1)}, bf16[4,512,512]{2,1,0:T(8,128)(2,1)}, s32[8,128]{1,0:T(8,128)}) custom-call(bf16[1024,128]{1,0:T(8,128)(2,1)} %wave.1, bf16[4,1024,512]{2,1,0:T(8,128)(2,1)} %row_ops.3, bf16[4,512,512]{2,1,0:T(8,128)(2,1)} %cols.1, s32[8,128]{1,0:T(8,128)} %pad.4.table), custom_call_target="tpu_custom_call" | custom-call | tf_op jit(solution)/shard_map/gather/pallas_call | solution.py:164
  39.0 0.0 copy-done.1
  39.0 0.0 copy-done.5
  39.0 0.0 copy-start.2
  39.0 1.6 %copy-done.2 = bf16[4,512,512]{2,1,0:T(8,128)(2,1)S(1)} copy-done((bf16[4,512,512]{2,1,0:T(8,128)(2,1)S(1)}, bf16[4,512,512]{2,1,0:T(8,128)(2,1)}, u32[]{:S(2)}) %copy-start.2) | copy-done | bytes 2097176
  40.6 0.0 copy-start.7
  40.6 0.7 copy-done.7
  41.3 7.0 %terms.1.part_h = bf16[16,512,256]{2,1,0:T(8,128)(2,1)} custom-call(s32[8,128]{1,0:T(8,128)S(1)} %copy-done.5, s32[8,128]{1,0:T(8,128)S(1)} %copy-done.7, bf16[4,1024,512]{2,1,0:T(8,128)(2,1)} %row_ops.3, bf16[4,512,512]{2,1,0:T(8,128)(2,1)S(1)} %copy-done.2, bf16[4,512,512]{2,1,0:T(8,128)(2,1)S(1)} %copy-done.1, ...), custom_call_target="tpu_custom_call" | custom-call | tf_op jit(solution)/shard_map/terms/pallas_call | solution.py:255
  48.3 74.3 %step.1 = (bf16[2,16,512,256]{3,2,1,0:T(8,128)(2,1)}, bf16[2,512,512]{2,1,0:T(8,128)(2,1)}, f32[2,8,128]{2,1,0:T(8,128)}, f32[1024,128]{1,0:T(8,128)}, f32[8,128]{1,0:T(8,128)}) custom-call(bf16[16,512,256]{2,1,0:T(8,128)(2,1)} %terms.1.part_h, bf16[16,512,256]{2,1,0:T(8,128)(2,1)} %get-tuple-element.17.wide.wide_h, f32[1024,1]{1,0:T(8,128)} %copy.10.energy_col), custom_call_target="tpu_custom_call" | custom-call | tf_op jit(solution)/shard_map/step/pallas_call | solution.py:526
  122.7 1.2 slice.3
  123.8 0.0 copy-start
  123.8 3.4 %copy-done = bf16[2,16,512,256]{3,2,1,0:T(8,128)(2,1)S(1)} copy-done((bf16[2,16,512,256]{3,2,1,0:T(8,128)(2,1)S(1)}, bf16[2,16,512,256]{3,2,1,0:T(8,128)(2,1)}, u32[]{:S(2)}) %copy-start) | copy-done | bytes 8388632
  127.2 0.0 copy-start.3
  127.2 1.2 copy-done.3
  128.5 0.0 copy-start.4
  128.5 1.0 copy-done.4
  129.5 0.0 copy-start.6
  129.5 0.7 copy-done.6
  130.2 8.2 %renorm.1 = (f32[4,1024,512]{2,1,0:T(8,128)}, f32[1024,128]{1,0:T(8,128)}) custom-call(s32[10]{0:T(128)S(1)} %pad_add_fusion.table, bf16[2,16,512,256]{3,2,1,0:T(8,128)(2,1)S(1)} %copy-done, bf16[2,16,512,256]{3,2,1,0:T(8,128)(2,1)S(1)} %copy-done, bf16[4,512,512]{2,1,0:T(8,128)(2,1)S(1)} %copy-done.1, bf16[2,512,512]{2,1,0:T(8,128)(2,1)S(1)} %copy-done.3, ...), custom_call_target="tpu_custom_call" | custom-call | tf_op jit(solution)/shard_map/renorm/pallas_call | solution.py:621
Async XLA Ops:
  0.6 38.4 %copy-start.1 = (bf16[4,512,512]{2,1,0:T(8,128)(2,1)S(1)}, bf16[4,512,512]{2,1,0:T(8,128)(2,1)}, u32[]{:S(2)}) copy-start(bf16[4,512,512]{2,1,0:T(8,128)(2,1)} %cols.1) | copy-start | bytes 6291460
  2.8 36.2 %copy-start.5 = (s32[8,128]{1,0:T(8,128)S(1)}, s32[8,128]{1,0:T(8,128)}, u32[]{:S(2)}) copy-start(s32[8,128]{1,0:T(8,128)} %pad.4.table) | copy-start | bytes 12292
  39.0 1.6 %copy-start.2 = (bf16[4,512,512]{2,1,0:T(8,128)(2,1)S(1)}, bf16[4,512,512]{2,1,0:T(8,128)(2,1)}, u32[]{:S(2)}) copy-start(bf16[4,512,512]{2,1,0:T(8,128)(2,1)} %get-tuple-element.15.row_sib) | copy-start | bytes 6291460
  40.6 0.7 copy-start.7
  123.8 3.4 %copy-start = (bf16[2,16,512,256]{3,2,1,0:T(8,128)(2,1)S(1)}, bf16[2,16,512,256]{3,2,1,0:T(8,128)(2,1)}, u32[]{:S(2)}) copy-start(bf16[2,16,512,256]{3,2,1,0:T(8,128)(2,1)} %get-tuple-element.18.src_block.tgt_block) | copy-start | bytes 25165828
  127.2 1.2 copy-start.3
  128.5 1.0 copy-start.4
  129.5 0.7 copy-start.6
where the time goes:
time: 141 us; the launch traced here: 138 us
  Pallas kernels  124 us (88%)
  local copies, waits for them, and re-layouts  12.1 us (9%)
  between operations  1.49 us (1%)
    pallas_call x1, Pallas kernels, step(): pl.pallas_call(step_kernel, out_shape=(jax.ShapeDtypeStruct((2, CHIPS, SE...  74.3 us
    pallas_call x1, Pallas kernels, gather(): pl.pallas_call(gather_kernel, out_shape=(jax.ShapeDtypeStruct((CHIPS, SEC...  34.5 us
    unnamed x16, local copies, waits for them, and re-layouts  8.61 us
    pallas_call x1, Pallas kernels, renorm(): pl.pallas_call(renorm_kernel, out_shape=(jax.ShapeDtypeStruct((4, 2 * SEC...  8.19 us
    pallas_call x1, Pallas kernels, terms(): pl.pallas_call(terms_kernel, out_shape=jax.ShapeDtypeStruct((CHIPS, SEC,...  7.03 us

commit v1 on v0

--- a/solution.py
+++ b/solution.py
@@ -127,7 +127,8 @@
 
 
 def gather_kernel(
-    wave, row_ops, col_ops, table, wide, row_sib, col_sib, table_sib, send, recv, swap_send, swap_recv, own_sem
+    wave, row_ops, col_ops, count, source, target, wide, row_sib, col_sib, table_sib,
+    table, send, recv, swap_send, swap_recv, own_sem,
 ):
     x, z, c = lax.axis_index("x"), lax.axis_index("z"), lax.axis_index("core")
     sib = {"core": 1 - c}
@@ -146,6 +147,12 @@
     ]
     swaps[0].start()
     own.start()
+    lane = lax.broadcasted_iota(jnp.int32, (8, 128), 1)
+    numbers = jnp.where(lane == 0, count[0], 0)
+    for k in range(4):
+        numbers = jnp.where(lane == 1 + k, source[k], numbers)
+        numbers = jnp.where(lane == 5 + k, target[k], numbers)
+    table[...] = numbers
     own.wait()
     push(wave.at[other, :], wide.at[b, :, other_columns], swap_send.at[0], swap_recv.at[0], sib).wait_recv()
     steps = all_blocks(wide, x, z, send, recv)
@@ -159,8 +166,9 @@
         swap.wait()
 
 
-def gather(wave, row_ops, col_ops, table):
-    hbm = pl.BlockSpec(memory_space=pl.ANY)
+def gather(wave, row_ops, col_ops, count, source, target):
+    hbm = pl.BlockSpec(memory_space=pltpu.HBM)
+    smem = pl.BlockSpec(memory_space=pltpu.SMEM)
     return pl.pallas_call(
         gather_kernel,
         out_shape=(
@@ -169,9 +177,10 @@
             jax.ShapeDtypeStruct((4, SEC, SEC), BF16),
             jax.ShapeDtypeStruct((8, 128), jnp.int32),
         ),
-        in_specs=[hbm] * 4,
+        in_specs=[hbm] * 3 + [smem] * 3,
         out_specs=(hbm,) * 4,
         scratch_shapes=[
+            pltpu.VMEM((8, 128), jnp.int32),
             pltpu.SemaphoreType.DMA((2, 20)),
             pltpu.SemaphoreType.DMA((2, 20)),
             pltpu.SemaphoreType.DMA((4,)),
@@ -180,7 +189,7 @@
         ],
         compiler_params=pltpu.CompilerParams(collective_id=0, has_side_effects=True),
         name="gather",
-    )(wave, row_ops, col_ops, table)
+    )(wave, row_ops, col_ops, count, source, target)
 
 
 def dot(a, b):
@@ -192,11 +201,12 @@
 
 
 def terms_kernel(
-    table, table_sib, row_ops, row_sib, col_ops, col_sib, wide, out, wide_v, row_v, col_v, total, wide_sem, row_sem, col_sem
+    count, source, target, table_sib, row_ops, row_sib, col_ops, col_sib, wide,
+    out, wide_v, row_v, col_v, total, wide_sem, row_sem, col_sem,
 ):
-    c = table[0, 9]
+    c = lax.axis_index("core")
     mine = pl.ds(pl.multiple_of(c * SEC, SEC), SEC)
-    counts = (table[0, 0], table_sib[0, 0])
+    counts = (count[0], table_sib[0, 0])
     load = pltpu.make_async_copy(wide, wide_v, wide_sem)
     load.start()
 
@@ -224,12 +234,11 @@
     lax.fori_loop(0, CHIPS, clear, 0)
     load.wait()
     for side in (0, 1):
-        this = (table, table_sib)[side]
-
-        def term(k, carry, side=side, this=this):
+
+        def term(k, carry, side=side):
             slot = side * 4 + k
-            src = this[0, 1 + k] * 2
-            tgt = this[0, 5 + k] * 2
+            src = (table_sib[0, 1 + k] if side else source[k]) * 2
+            tgt = (table_sib[0, 5 + k] if side else target[k]) * 2
             for one in copies(side, k):
                 one.wait()
             rows = row_v[slot]
@@ -249,13 +258,13 @@
     lax.fori_loop(0, CHIPS, finish, 0)
 
 
-def terms(table, table_sib, row_ops, row_sib, col_ops, col_sib, wide):
-    hbm = pl.BlockSpec(memory_space=pl.ANY)
+def terms(count, source, target, table_sib, row_ops, row_sib, col_ops, col_sib, wide):
+    hbm = pl.BlockSpec(memory_space=pltpu.HBM)
     smem = pl.BlockSpec(memory_space=pltpu.SMEM)
     return pl.pallas_call(
         terms_kernel,
         out_shape=jax.ShapeDtypeStruct((CHIPS, SEC, WIDE), BF16),
-        in_specs=[smem, smem] + [hbm] * 5,
+        in_specs=[smem] * 4 + [hbm] * 5,
         out_specs=pl.BlockSpec(memory_space=pltpu.VMEM),
         scratch_shapes=[
             pltpu.VMEM((CHIPS, SEC, WIDE), BF16),
@@ -266,9 +275,9 @@
             pltpu.SemaphoreType.DMA((8,)),
             pltpu.SemaphoreType.DMA((8,)),
         ],
-        compiler_params=pltpu.CompilerParams(vmem_limit_bytes=48 * MIB),
+        compiler_params=pltpu.CompilerParams(vmem_limit_bytes=60 * MIB),
         name="terms",
-    )(table, table_sib, row_ops, row_sib, col_ops, col_sib, wide)
+    )(count, source, target, table_sib, row_ops, row_sib, col_ops, col_sib, wide)
 
 
 def rough(a, b):
@@ -383,9 +392,9 @@
 
 
 def step_kernel(
-    part_h, wide_h, energy_col,
+    part_h, wide_h, energy_row,
     stepped_o, root_o, level_o, exact_o, energy_o,
-    part, near, whole, near2, whole2, total, wide, summed, stepped, gram, my, mm, mu, mz, roots, level_two, exact, scalars,
+    part, near, whole, near2, whole2, total, wide, summed, stepped, gram, my, mm, mu, mz, roots, level_two, exact, scalars, energy_col,
     rs_send, rs_recv, rs2_send, rs2_recv, ag_send, ag_recv, en_send, en_recv, st_send, st_recv, st_own,
     end_send, end_recv, own_sem,
 ):
@@ -399,6 +408,10 @@
         ring_peers(x, z)
         + [{"x": turn(x, 2)}, {"z": turn(z, 2)}, sib, {"sec": turn(y, 1)}, {"sec": turn(y, 2)}, {"sec": turn(y, -1)}]
     )
+    same = lax.broadcasted_iota(jnp.int32, (128, 128), 0) == lax.broadcasted_iota(jnp.int32, (128, 128), 1)
+    for i in range(4):
+        spread = jnp.where(same, jnp.broadcast_to(energy_row[pl.ds(c * 4 + i, 1), :], (128, 128)), 0.0)
+        energy_col[pl.ds(i * 128, 128), :] = jnp.sum(spread, axis=1, keepdims=True)
     load.wait()
     load_wide.start()
     reduce_blocks(part, near, whole, near2, whole2, total, x, z, rs_send, rs_recv, rs2_send, rs2_recv)
@@ -406,7 +419,7 @@
     steps = all_blocks(summed, x, z, ag_send, ag_recv)
     next(steps)
     load_wide.wait()
-    level = energy_col[pl.ds(pl.multiple_of(c * SEC, SEC), SEC), :]
+    level = energy_col[...]
     amplitude = wide[b].astype(F32)
     applied = level * amplitude + total[...]
     share = jnp.sum(amplitude * applied, axis=(0, 1), keepdims=True)
@@ -517,8 +530,8 @@
     push(level_two, level_o.at[1 - c], end_send.at[2], end_recv.at[2], sib).wait_recv()
 
 
-def step(part, wide, energy_col):
-    hbm = pl.BlockSpec(memory_space=pl.ANY)
+def step(part, wide, energy_row):
+    hbm = pl.BlockSpec(memory_space=pltpu.HBM)
     vmem = pl.BlockSpec(memory_space=pltpu.VMEM)
     square = pltpu.VMEM((SEC, SEC), F32)
     blocks = pltpu.VMEM((CHIPS, SEC, WIDE), BF16)
@@ -553,6 +566,7 @@
             pltpu.VMEM((8, 128), F32),
             pltpu.VMEM((2, SEC, 128), F32),
             pltpu.VMEM((4, 4, 8, 128), F32),
+            pltpu.VMEM((SEC, 1), F32),
             dma((2, 6, 4)),
             dma((2, 6, 4)),
             dma((2, 6)),
@@ -569,21 +583,22 @@
             dma((5,)),
         ],
         compiler_params=pltpu.CompilerParams(
-            collective_id=1, has_side_effects=True, vmem_limit_bytes=56 * MIB
+            collective_id=1, has_side_effects=True, vmem_limit_bytes=60 * MIB
         ),
         name="step",
-    )(part, wide, energy_col)
-
-
-def renorm_kernel(table, src_block, tgt_block, cols, root, level, exact, out, wave_o):
+    )(part, wide, energy_row)
+
+
+def renorm_kernel(count, source, target, src_block, tgt_block, cols, root, level, exact, energy, out, wave_o, energy_o):
     k = pl.program_id(0)
     scale = level[0, 0:1, 0:1]
 
     @pl.when(k == 0)
     def first():
+        energy_o[0] = energy[0, 0]
         wave_o[...] = scale * exact[...] + dot(root[0], exact[...].astype(BF16))
 
-    @pl.when(k < table[0])
+    @pl.when(k < count[0])
     def live():
         product = None
         for part in (0, 1):
@@ -600,60 +615,72 @@
             total = added if total is None else total + added
         out[0] = total * SEC ** (-0.5)
 
-    @pl.when(k >= table[0])
+    @pl.when(k >= count[0])
     def empty():
         out[...] = jnp.zeros_like(out)
 
 
-def renorm(table, stepped, cols, root, level, exact):
-    def slot(k, table):
-        return jnp.minimum(k, table[0] - 1)
-
-    def sector(k, s, table):
-        return jnp.where(k < table[0], s, 1)
-
-    def src_at(k, s, table):
-        return (sector(k, s, table), table[1 + slot(k, table)], 0, 0)
-
-    def tgt_at(k, s, table):
-        return (sector(k, s, table), table[5 + slot(k, table)], 0, 0)
+def renorm(count, source, target, stepped, cols, root, level, exact, energy):
+    def slot(k, count):
+        return jnp.minimum(k, count[0] - 1)
+
+    def sector(k, s, count):
+        return jnp.where(k < count[0], s, 1)
+
+    def src_at(k, s, count, source, target):
+        return (sector(k, s, count), source[slot(k, count)], 0, 0)
+
+    def tgt_at(k, s, count, source, target):
+        return (sector(k, s, count), target[slot(k, count)], 0, 0)
+
+    def root_at(k, s, count, source, target):
+        return (sector(k, s, count), 0, 0)
+
+    def once_at(k, s, count, source, target):
+        return (jnp.where(k == 0, s, 1), 0)
 
     return pl.pallas_call(
         renorm_kernel,
         out_shape=(
             jax.ShapeDtypeStruct((4, 2 * SEC, SEC), F32),
             jax.ShapeDtypeStruct((2 * SEC, 128), F32),
+            jax.ShapeDtypeStruct((1,), F32),
         ),
         grid_spec=pltpu.PrefetchScalarGridSpec(
-            num_scalar_prefetch=1,
+            num_scalar_prefetch=3,
             grid=(4, 2),
             in_specs=[
                 pl.BlockSpec((1, 2, SEC, WIDE), src_at),
                 pl.BlockSpec((1, 2, SEC, WIDE), tgt_at),
-                pl.BlockSpec((1, SEC, SEC), lambda k, s, table: (slot(k, table), 0, 0)),
-                pl.BlockSpec((1, SEC, SEC), lambda k, s, table: (sector(k, s, table), 0, 0)),
-                pl.BlockSpec((1, 8, 128), lambda k, s, table: (sector(k, s, table), 0, 0)),
-                pl.BlockSpec((SEC, 128), lambda k, s, table: (jnp.where(k == 0, s, 1), 0)),
+                pl.BlockSpec((1, SEC, SEC), lambda k, s, count, source, target: (slot(k, count), 0, 0)),
+                pl.BlockSpec((1, SEC, SEC), root_at),
+                pl.BlockSpec((1, 8, 128), root_at),
+                pl.BlockSpec((SEC, 128), once_at),
+                pl.BlockSpec(memory_space=pltpu.SMEM),
             ],
             out_specs=[
-                pl.BlockSpec((1, SEC, SEC), lambda k, s, table: (k, s, 0)),
-                pl.BlockSpec((SEC, 128), lambda k, s, table: (jnp.where(k == 0, s, 1), 0)),
+                pl.BlockSpec((1, SEC, SEC), lambda k, s, count, source, target: (k, s, 0)),
+                pl.BlockSpec((SEC, 128), once_at),
+                pl.BlockSpec(memory_space=pltpu.SMEM),
             ],
         ),
-        compiler_params=pltpu.CompilerParams(vmem_limit_bytes=32 * MIB),
+        compiler_params=pltpu.CompilerParams(vmem_limit_bytes=60 * MIB),
         name="renorm",
-    )(table, stepped, stepped, cols, root, level, exact)
+    )(count, source, target, stepped, stepped, cols, root, level, exact, energy)
 
 
 def on_device(wave_in, row_energy, row_operators, column_operators, term_count, source, target):
-    core = lax.axis_index("core").astype(jnp.int32).reshape(1)
-    numbers = jnp.concatenate([term_count, source, target, core])
-    table = jnp.pad(numbers.reshape(1, 10), ((0, 7), (0, 118)))
-    wide, row_sib, col_sib, table_sib = gather(wave_in, row_operators, column_operators, table)
-    part = terms(table, table_sib, row_operators, row_sib, column_operators, col_sib, wide)
-    stepped, root, level, exact, energy = step(part, wide, row_energy.reshape(-1, 1))
-    renormalized, wave_next = renorm(numbers, stepped, column_operators, root, level, exact)
-    return (wave_next, renormalized, energy[0, 0])
+    wide, row_sib, col_sib, table_sib = gather(
+        wave_in, row_operators, column_operators, term_count, source, target
+    )
+    part = terms(
+        term_count, source, target, table_sib, row_operators, row_sib, column_operators, col_sib, wide
+    )
+    stepped, root, level, exact, energy = step(part, wide, row_energy.reshape(8, 128))
+    renormalized, wave_next, energy = renorm(
+        term_count, source, target, stepped, column_operators, root, level, exact, energy
+    )
+    return (wave_next, renormalized, energy.reshape(()))
 
 
 def solution(mesh):

time: 141 us -> 133 us (0.943)
  the two profiles are of different devices: /device:TPU:1 before, /device:TPU:20 now
where the time goes in v1:
time: 133 us
  Pallas kernels  132 us (99%)
    pallas_call x1, Pallas kernels, step(): pl.pallas_call(step_kernel, out_shape=(jax.ShapeDtypeStruct((2, CHIPS, SE...  68.5 us
    pallas_call x1, Pallas kernels, gather(): pl.pallas_call(gather_kernel, out_shape=(jax.ShapeDtypeStruct((CHIPS, SEC...  35.6 us
    pallas_call x1, Pallas kernels, renorm(): pl.pallas_call(renorm_kernel, out_shape=(jax.ShapeDtypeStruct((4, 2 * SEC...  16.7 us
    pallas_call x1, Pallas kernels, terms(): pl.pallas_call(terms_kernel, out_shape=jax.ShapeDtypeStruct((CHIPS, SEC,...  10.8 us

profile of v1, /device:TPU:20, one launch (start us, length us, event | category | flops | bytes accessed | tf_op | source)
XLA Modules:
  0.0 132.9 jit_solution(4193712413346210971)
XLA Ops:
  1.3 35.6 %gather.1 = (bf16[16,512,256]{2,1,0:T(8,128)(2,1)}, bf16[4,512,512]{2,1,0:T(8,128)(2,1)}, bf16[4,512,512]{2,1,0:T(8,128)(2,1)}, s32[8,128]{1,0:T(8,128)}) custom-call(bf16[1024,128]{1,0:T(8,128)(2,1)} %wave.1, bf16[4,1024,512]{2,1,0:T(8,128)(2,1)} %row_ops.3, bf16[4,512,512]{2,1,0:T(8,128)(2,1)} %cols.1, s32[1]{0:T(128)S(6)} %copy.10.count, s32[4]{0:T(128)} %source.5, ...), custom_call_target="tpu_custom_call" | custom-call | tf_op jit(solution)/shard_map/gather/pallas_call | solution.py:172
  36.9 10.8 %terms.1.part_h = bf16[16,512,256]{2,1,0:T(8,128)(2,1)} custom-call(s32[1]{0:T(128)S(6)} %copy.10.count, s32[4]{0:T(128)} %source.5, s32[4]{0:T(128)} %target.5, s32[8,128]{1,0:T(8,128)} %get-tuple-element.15.table_sib, bf16[4,1024,512]{2,1,0:T(8,128)(2,1)} %row_ops.3, bf16[4,512,512]{2,1,0:T(8,128)(2,1)} %get-tuple-element.16.row_sib, ...), custom_call_target="tpu_custom_call" | custom-call | tf_op jit(solution)/shard_map/terms/pallas_call | solution.py:264
  47.6 68.5 %step.1 = (bf16[2,16,512,256]{3,2,1,0:T(8,128)(2,1)}, bf16[2,512,512]{2,1,0:T(8,128)(2,1)}, f32[2,8,128]{2,1,0:T(8,128)}, f32[1024,128]{1,0:T(8,128)}, f32[8,128]{1,0:T(8,128)}) custom-call(bf16[16,512,256]{2,1,0:T(8,128)(2,1)} %terms.1.part_h, bf16[16,512,256]{2,1,0:T(8,128)(2,1)} %get-tuple-element.18.wide.wide_h, f32[8,128]{1,0:T(8,128)} %bitcast.2), custom_call_target="tpu_custom_call" | custom-call | tf_op jit(solution)/shard_map/step/pallas_call | solution.py:539
  116.2 16.7 %renorm.1 = (f32[4,1024,512]{2,1,0:T(8,128)}, f32[1024,128]{1,0:T(8,128)}, f32[1]{0:T(128)}) custom-call(s32[1]{0:T(128)S(6)} %copy.10.count, s32[4]{0:T(128)} %source.5, s32[4]{0:T(128)} %target.5, bf16[2,16,512,256]{3,2,1,0:T(8,128)(2,1)} %get-tuple-element.19.src_block.tgt_block, bf16[2,16,512,256]{3,2,1,0:T(8,128)(2,1)} %get-tuple-element.19.src_block.tgt_block, ...), custom_call_target="tpu_custom_call" | custom-call | tf_op jit(solution)/shard_map/renorm/pallas_call | solution.py:642

commit v2 on v1

--- a/solution.py
+++ b/solution.py
@@ -100,7 +100,7 @@
 
     for h in (0, 1):
         onward(h, 0)
-    yield
+    yield 1
     for h in (0, 1):
         p, q = places[h]
         far = turn(p, 2)
@@ -109,15 +109,28 @@
         go(h, 7, far, q, None, 1, 1)
         go(h, 11, far, q, None, 1, -1)
     yield
-    for i in (1, 2, 3):
-        for h in (0, 1):
-            onward(h, i)
-        yield
-    for i in range(4):
+    for h in (0, 1):
+        onward(h, 1)
+    yield
+    for h in (0, 1):
+        onward(h, 2)
+    yield 2
+
+    def last(i):
         for h in (0, 1):
             pa, far = order(h)[i], turn(places[h][1], 2)
             arrived(h, 12 + i, pa, far, 0)
             arrived(h, 16 + i, pa, far, 1)
+
+    last(0)
+    yield 3
+    for h in (0, 1):
+        onward(h, 3)
+    last(1)
+    last(2)
+    yield 4
+    last(3)
+    yield 5
     for one in sent:
         one.wait_send()
 
@@ -126,158 +139,12 @@
     return [{"x": turn(x, 1)}, {"x": turn(x, -1)}, {"z": turn(z, 1)}, {"z": turn(z, -1)}]
 
 
-def gather_kernel(
-    wave, row_ops, col_ops, count, source, target, wide, row_sib, col_sib, table_sib,
-    table, send, recv, swap_send, swap_recv, own_sem,
-):
-    x, z, c = lax.axis_index("x"), lax.axis_index("z"), lax.axis_index("core")
-    sib = {"core": 1 - c}
-    greet(ring_peers(x, z) + [sib])
-    b = x * 4 + z
-    mine = pl.ds(pl.multiple_of(c * SEC, SEC), SEC)
-    other = pl.ds(pl.multiple_of((1 - c) * SEC, SEC), SEC)
-    columns = pl.ds(pl.multiple_of(c * 128, 128), 128)
-    other_columns = pl.ds(pl.multiple_of((1 - c) * 128, 128), 128)
-    own = pltpu.make_async_copy(wave.at[mine, :], wide.at[b, :, columns], own_sem)
-    swaps = [
-        push(wave.at[other, :], wide.at[b, :, columns], swap_send.at[0], swap_recv.at[0], sib),
-        push(table, table_sib, swap_send.at[1], swap_recv.at[1], sib),
-        push(row_ops.at[:, other, :], row_sib, swap_send.at[2], swap_recv.at[2], sib),
-        push(col_ops, col_sib, swap_send.at[3], swap_recv.at[3], sib),
-    ]
-    swaps[0].start()
-    own.start()
-    lane = lax.broadcasted_iota(jnp.int32, (8, 128), 1)
-    numbers = jnp.where(lane == 0, count[0], 0)
-    for k in range(4):
-        numbers = jnp.where(lane == 1 + k, source[k], numbers)
-        numbers = jnp.where(lane == 5 + k, target[k], numbers)
-    table[...] = numbers
-    own.wait()
-    push(wave.at[other, :], wide.at[b, :, other_columns], swap_send.at[0], swap_recv.at[0], sib).wait_recv()
-    steps = all_blocks(wide, x, z, send, recv)
-    next(steps)
-    for swap in swaps[1:]:
-        swap.start()
-    for step in steps:
-        del step
-    swaps[0].wait_send()
-    for swap in swaps[1:]:
-        swap.wait()
-
-
-def gather(wave, row_ops, col_ops, count, source, target):
-    hbm = pl.BlockSpec(memory_space=pltpu.HBM)
-    smem = pl.BlockSpec(memory_space=pltpu.SMEM)
-    return pl.pallas_call(
-        gather_kernel,
-        out_shape=(
-            jax.ShapeDtypeStruct((CHIPS, SEC, WIDE), BF16),
-            jax.ShapeDtypeStruct((4, SEC, SEC), BF16),
-            jax.ShapeDtypeStruct((4, SEC, SEC), BF16),
-            jax.ShapeDtypeStruct((8, 128), jnp.int32),
-        ),
-        in_specs=[hbm] * 3 + [smem] * 3,
-        out_specs=(hbm,) * 4,
-        scratch_shapes=[
-            pltpu.VMEM((8, 128), jnp.int32),
-            pltpu.SemaphoreType.DMA((2, 20)),
-            pltpu.SemaphoreType.DMA((2, 20)),
-            pltpu.SemaphoreType.DMA((4,)),
-            pltpu.SemaphoreType.DMA((4,)),
-            pltpu.SemaphoreType.DMA(()),
-        ],
-        compiler_params=pltpu.CompilerParams(collective_id=0, has_side_effects=True),
-        name="gather",
-    )(wave, row_ops, col_ops, count, source, target)
-
-
 def dot(a, b):
     return jnp.dot(a, b, preferred_element_type=F32)
 
 
 def dot_t(a, b):
     return lax.dot_general(a, b, (((1,), (1,)), ((), ())), preferred_element_type=F32)
-
-
-def terms_kernel(
-    count, source, target, table_sib, row_ops, row_sib, col_ops, col_sib, wide,
-    out, wide_v, row_v, col_v, total, wide_sem, row_sem, col_sem,
-):
-    c = lax.axis_index("core")
-    mine = pl.ds(pl.multiple_of(c * SEC, SEC), SEC)
-    counts = (count[0], table_sib[0, 0])
-    load = pltpu.make_async_copy(wide, wide_v, wide_sem)
-    load.start()
-
-    def copies(side, k):
-        slot = side * 4 + k
-        rows = (row_ops.at[k, mine, :], row_sib.at[k])[side]
-        cols = (col_ops.at[k], col_sib.at[k])[side]
-        return (
-            pltpu.make_async_copy(rows, row_v.at[slot], row_sem.at[slot]),
-            pltpu.make_async_copy(cols, col_v.at[slot], col_sem.at[slot]),
-        )
-
-    for k in range(4):
-        for side in (0, 1):
-
-            @pl.when(k < counts[side])
-            def start(side=side, k=k):
-                for one in copies(side, k):
-                    one.start()
-
-    def clear(i, carry):
-        total[i] = jnp.zeros((SEC, WIDE), F32)
-        return carry
-
-    lax.fori_loop(0, CHIPS, clear, 0)
-    load.wait()
-    for side in (0, 1):
-
-        def term(k, carry, side=side):
-            slot = side * 4 + k
-            src = (table_sib[0, 1 + k] if side else source[k]) * 2
-            tgt = (table_sib[0, 5 + k] if side else target[k]) * 2
-            for one in copies(side, k):
-                one.wait()
-            rows = row_v[slot]
-            first = dot(rows, wide_v[src]).astype(BF16)
-            second = dot(rows, wide_v[src + 1]).astype(BF16)
-            for part in (0, 1):
-                where = pl.ds(part * WIDE, WIDE)
-                total[tgt + part] += dot(first, col_v[slot, :WIDE, where]) + dot(second, col_v[slot, WIDE:, where])
-            return carry
-
-        lax.fori_loop(0, counts[side], term, 0)
-
-    def finish(i, carry):
-        out[i] = total[i].astype(BF16)
-        return carry
-
-    lax.fori_loop(0, CHIPS, finish, 0)
-
-
-def terms(count, source, target, table_sib, row_ops, row_sib, col_ops, col_sib, wide):
-    hbm = pl.BlockSpec(memory_space=pltpu.HBM)
-    smem = pl.BlockSpec(memory_space=pltpu.SMEM)
-    return pl.pallas_call(
-        terms_kernel,
-        out_shape=jax.ShapeDtypeStruct((CHIPS, SEC, WIDE), BF16),
-        in_specs=[smem] * 4 + [hbm] * 5,
-        out_specs=pl.BlockSpec(memory_space=pltpu.VMEM),
-        scratch_shapes=[
-            pltpu.VMEM((CHIPS, SEC, WIDE), BF16),
-            pltpu.VMEM((8, SEC, SEC), BF16),
-            pltpu.VMEM((8, SEC, SEC), BF16),
-            pltpu.VMEM((CHIPS, SEC, WIDE), F32),
-            pltpu.SemaphoreType.DMA(()),
-            pltpu.SemaphoreType.DMA((8,)),
-            pltpu.SemaphoreType.DMA((8,)),
-        ],
-        compiler_params=pltpu.CompilerParams(vmem_limit_bytes=60 * MIB),
-        name="terms",
-    )(count, source, target, table_sib, row_ops, row_sib, col_ops, col_sib, wide)
 
 
 def rough(a, b):
@@ -391,34 +258,131 @@
     return jnp.sqrt(jnp.sum(a * a, axis=(0, 1), keepdims=True) + 1e-06)
 
 
-def step_kernel(
-    part_h, wide_h, energy_row,
+def group_block(group, t, x, z):
+    if group == 1:
+        dx = (t == 1).astype(jnp.int32) - (t == 2).astype(jnp.int32)
+        dz = (t == 3).astype(jnp.int32) - (t == 4).astype(jnp.int32)
+    elif group == 2:
+        dx, dz = 1 - 2 * lax.rem(t, 2), 1 - 2 * lax.div(t, 2)
+    elif group == 3:
+        dx, dz = 2 - 2 * t, 2 * t
+    elif group == 4:
+        dx, dz = jnp.where(t < 2, 1 - 2 * t, 2), jnp.where(t < 2, 2, 5 - 2 * t)
+    else:
+        dx = dz = 2
+    return turn(x, dx) * 4 + turn(z, dz)
+
+
+GROUP_SIZE = {1: 5, 2: 4, 3: 2, 4: 4, 5: 1}
+
+
+def site_kernel(
+    wave, row_ops, col_ops, count, source, target, energy_row,
     stepped_o, root_o, level_o, exact_o, energy_o,
-    part, near, whole, near2, whole2, total, wide, summed, stepped, gram, my, mm, mu, mz, roots, level_two, exact, scalars, energy_col,
+    wide, row_v, col_v, table, table_in, table_s, order_s, source_s, prefix,
+    part, near, whole, near2, whole2, total, summed, stepped, gram, my, mm, mu, mz, roots, level_two, exact, scalars, energy_col,
+    wv_send, wv_recv, swap_send, swap_recv,
     rs_send, rs_recv, rs2_send, rs2_recv, ag_send, ag_recv, en_send, en_recv, st_send, st_recv, st_own,
     end_send, end_recv, own_sem,
 ):
     x, z, c, y = lax.axis_index("x"), lax.axis_index("z"), lax.axis_index("core"), lax.axis_index("sec")
     b = x * 4 + z
     sib = {"core": 1 - c}
-    load = pltpu.make_async_copy(part_h, part, own_sem.at[0])
-    load_wide = pltpu.make_async_copy(wide_h, wide, own_sem.at[1])
-    load.start()
+    mine = pl.ds(pl.multiple_of(c * SEC, SEC), SEC)
+    other = pl.ds(pl.multiple_of((1 - c) * SEC, SEC), SEC)
+    columns = pl.ds(pl.multiple_of(c * 128, 128), 128)
+    other_columns = pl.ds(pl.multiple_of((1 - c) * 128, 128), 128)
+    own_slots, sib_slots = pl.ds(0, 4), pl.ds(4, 4)
+    own_wave = pltpu.make_async_copy(wave.at[mine, :], wide.at[b, :, columns], own_sem.at[0])
+    own_wave.start()
+    lane = lax.broadcasted_iota(jnp.int32, (8, 128), 1)
+    numbers = jnp.where(lane == 0, count[0], 0)
+    for k in range(4):
+        numbers = jnp.where(lane == 1 + k, source[k], numbers)
+        numbers = jnp.where(lane == 5 + k, target[k], numbers)
+    table[...] = numbers
     greet(
         ring_peers(x, z)
-        + [{"x": turn(x, 2)}, {"z": turn(z, 2)}, sib, {"sec": turn(y, 1)}, {"sec": turn(y, 2)}, {"sec": turn(y, -1)}]
+        + [sib, {"x": turn(x, 2)}, {"z": turn(z, 2)}, {"sec": turn(y, 1)}, {"sec": turn(y, 2)}, {"sec": turn(y, -1)}]
     )
+    swaps = [
+        push(wave.at[other, :], wide.at[b, :, columns], swap_send.at[0], swap_recv.at[0], sib),
+        push(table, table_in, swap_send.at[1], swap_recv.at[1], sib),
+        push(row_ops.at[:, other, :], row_v.at[sib_slots], swap_send.at[2], swap_recv.at[2], sib),
+        push(col_ops, col_v.at[sib_slots], swap_send.at[3], swap_recv.at[3], sib),
+    ]
+    swaps[0].start()
+    own_wave.wait()
+    push(wave.at[other, :], wide.at[b, :, other_columns], swap_send.at[0], swap_recv.at[0], sib).wait_recv()
+    steps = all_blocks(wide, x, z, wv_send, wv_recv)
+    next(steps)
+    for swap in swaps[1:]:
+        swap.start()
+    own_rows = pltpu.make_async_copy(row_ops.at[:, mine, :], row_v.at[own_slots], own_sem.at[1])
+    own_cols = pltpu.make_async_copy(col_ops, col_v.at[own_slots], own_sem.at[5])
+    own_rows.start()
+    own_cols.start()
     same = lax.broadcasted_iota(jnp.int32, (128, 128), 0) == lax.broadcasted_iota(jnp.int32, (128, 128), 1)
     for i in range(4):
         spread = jnp.where(same, jnp.broadcast_to(energy_row[pl.ds(c * 4 + i, 1), :], (128, 128)), 0.0)
         energy_col[pl.ds(i * 128, 128), :] = jnp.sum(spread, axis=1, keepdims=True)
-    load.wait()
-    load_wide.start()
+    swaps[1].wait_recv()
+    to_scalars = pltpu.make_async_copy(table_in, table_s, own_sem.at[6])
+    to_scalars.start()
+    to_scalars.wait()
+
+    def flag(condition):
+        return condition.astype(jnp.int32)
+
+    keys, sources = [], []
+    for side in (0, 1):
+        live = table_s[0, 0] if side else count[0]
+        for k in range(4):
+            alive = flag(k < live)
+            aim = table_s[0, 5 + k] if side else target[k]
+            keys.append(aim * alive + 8 * (1 - alive))
+            sources.append(table_s[0, 1 + k] if side else source[k])
+    ranks = []
+    for i in range(8):
+        ahead = [flag(keys[j] <= keys[i]) if j < i else flag(keys[j] < keys[i]) for j in range(8) if j != i]
+        ranks.append(sum(ahead))
+    for j in range(8):
+        order_s[j] = sum(i * flag(ranks[i] == j) for i in range(8))
+        source_s[j] = sum(sources[i] * flag(ranks[i] == j) for i in range(8))
+    starts = [sum(flag(key < t) for key in keys) for t in range(9)]
+
+    for ready in steps:
+        del ready
+    swaps[0].wait_send()
+    swaps[1].wait_send()
+    own_rows.wait()
+    own_cols.wait()
+    swaps[2].wait()
+    swaps[3].wait()
+
+    prefix[0] = jnp.zeros((HALF, SEC), F32)
+    for h in (0, 1):
+        here = pl.ds(h * HALF, HALF)
+
+        def term(j, carry, here=here):
+            slot = order_s[j]
+            src = source_s[j] * 2
+            rows = row_v[slot, here, :]
+            first = dot(rows, wide[src]).astype(BF16)
+            second = dot(rows, wide[src + 1]).astype(BF16)
+            prefix[j + 1] = prefix[j] + (dot(first, col_v[slot, :WIDE, :]) + dot(second, col_v[slot, WIDE:, :]))
+            return carry
+
+        lax.fori_loop(0, 8, term, 0)
+        for t in range(8):
+            added = (prefix[starts[t + 1]] - prefix[starts[t]]).astype(BF16)
+            part[2 * t, here, :] = added[:, :WIDE]
+            part[2 * t + 1, here, :] = added[:, WIDE:]
+
     reduce_blocks(part, near, whole, near2, whole2, total, x, z, rs_send, rs_recv, rs2_send, rs2_recv)
     summed[b] = total[...].astype(BF16)
     steps = all_blocks(summed, x, z, ag_send, ag_recv)
     next(steps)
-    load_wide.wait()
     level = energy_col[...]
     amplitude = wide[b].astype(F32)
     applied = level * amplitude + total[...]
@@ -436,12 +400,14 @@
                 push(scalars.at[s, src], scalars.at[s, src], en_send.at[s, hop], en_recv.at[s, hop], to),
             )
 
+    groups = []
     for s in range(4):
         place, size = stages[s][1:]
         scalars[s, place] = jnp.broadcast_to(share, (8, 128))
         for out, unused in energy_copies(s):
             out.start()
-        next(steps, None)
+        ready = next(steps)
+        groups += [ready] if ready else []
         for out, arriving in energy_copies(s):
             arriving.wait_recv()
             out.wait_send()
@@ -451,13 +417,9 @@
         share = share[0:1, 0:1]
     energy = share * (1.0 / ENTRIES)
     energy_o[...] = jnp.broadcast_to(energy, (8, 128))
-    for step in steps:
-        del step
-
     own = amplitude + 0.5 * (energy * amplitude - applied)
     exact[0] = own[:, :128]
     exact[1] = own[:, 128:]
-    mine = pl.ds(pl.multiple_of(c * SEC, SEC), SEC)
     exact_send = push(exact.at[1 - c], exact_o.at[mine, :], end_send.at[0], end_recv.at[0], sib)
     exact_own = pltpu.make_async_copy(exact.at[c], exact_o.at[mine, :], own_sem.at[2])
     exact_send.start()
@@ -471,17 +433,25 @@
 
     gram[...] = jnp.zeros((SEC, SEC), F32)
 
-    def one_block(i, carry):
-        part_of = wide[i].astype(F32)
-        value = part_of + 0.5 * (energy * part_of - (level * part_of + summed[i].astype(F32)))
-        value = value.astype(BF16)
-        stepped[i] = value
-        for one in out_block(i):
-            one.start()
-        gram[...] += dot_t(value, value)
-        return carry
-
-    lax.fori_loop(0, CHIPS, one_block, 0)
+    def add_group(group):
+        def one_block(t, carry):
+            i = group_block(group, t, x, z)
+            part_of = wide[i].astype(F32)
+            value = part_of + 0.5 * (energy * part_of - (level * part_of + summed[i].astype(F32)))
+            value = value.astype(BF16)
+            stepped[i] = value
+            for one in out_block(i):
+                one.start()
+            gram[...] += dot_t(value, value)
+            return carry
+
+        lax.fori_loop(0, GROUP_SIZE[group], one_block, 0)
+
+    for group in groups:
+        add_group(group)
+    for ready in steps:
+        if ready:
+            add_group(ready)
 
     def root(y_ref, d_ref, again):
         my[...] = 1.5 * y_ref[...] - 0.5 * rough(y_ref[...], y_ref[...])
@@ -518,7 +488,6 @@
         return carry
 
     lax.fori_loop(0, CHIPS, block_done, 0)
-    other = pl.ds(pl.multiple_of((1 - c) * SEC, SEC), SEC)
     exact_send.wait_send()
     exact_own.wait()
     push(exact.at[1 - c], exact_o.at[other, :], end_send.at[0], end_recv.at[0], sib).wait_recv()
@@ -530,14 +499,15 @@
     push(level_two, level_o.at[1 - c], end_send.at[2], end_recv.at[2], sib).wait_recv()
 
 
-def step(part, wide, energy_row):
+def site(wave, row_ops, col_ops, count, source, target, energy_row):
     hbm = pl.BlockSpec(memory_space=pltpu.HBM)
+    smem = pl.BlockSpec(memory_space=pltpu.SMEM)
     vmem = pl.BlockSpec(memory_space=pltpu.VMEM)
     square = pltpu.VMEM((SEC, SEC), F32)
     blocks = pltpu.VMEM((CHIPS, SEC, WIDE), BF16)
     dma = pltpu.SemaphoreType.DMA
     return pl.pallas_call(
-        step_kernel,
+        site_kernel,
         out_shape=(
             jax.ShapeDtypeStruct((2, CHIPS, SEC, WIDE), BF16),
             jax.ShapeDtypeStruct((2, SEC, SEC), BF16),
@@ -545,16 +515,24 @@
             jax.ShapeDtypeStruct((2 * SEC, 128), F32),
             jax.ShapeDtypeStruct((8, 128), F32),
         ),
-        in_specs=[hbm, hbm, vmem],
+        in_specs=[hbm] * 3 + [smem] * 3 + [vmem],
         out_specs=(hbm, hbm, hbm, hbm, vmem),
         scratch_shapes=[
+            blocks,
+            pltpu.VMEM((8, SEC, SEC), BF16),
+            pltpu.VMEM((8, SEC, SEC), BF16),
+            pltpu.VMEM((8, 128), jnp.int32),
+            pltpu.VMEM((8, 128), jnp.int32),
+            pltpu.SMEM((8, 128), jnp.int32),
+            pltpu.SMEM((8,), jnp.int32),
+            pltpu.SMEM((8,), jnp.int32),
+            pltpu.VMEM((9, HALF, SEC), F32),
             blocks,
             pltpu.VMEM((2, 2, 4, QUARTER, WIDE), BF16),
             pltpu.VMEM((2, 2, 4, HALF, WIDE), BF16),
             pltpu.VMEM((2, 2, QUARTER, WIDE), BF16),
             pltpu.VMEM((2, 2, HALF, WIDE), BF16),
             pltpu.VMEM((SEC, WIDE), F32),
-            blocks,
             blocks,
             blocks,
             square,
@@ -567,6 +545,10 @@
             pltpu.VMEM((2, SEC, 128), F32),
             pltpu.VMEM((4, 4, 8, 128), F32),
             pltpu.VMEM((SEC, 1), F32),
+            dma((2, 20)),
+            dma((2, 20)),
+            dma((4,)),
+            dma((4,)),
             dma((2, 6, 4)),
             dma((2, 6, 4)),
             dma((2, 6)),
@@ -580,13 +562,13 @@
             dma((CHIPS,)),
             dma((3,)),
             dma((3,)),
-            dma((5,)),
+            dma((7,)),
         ],
         compiler_params=pltpu.CompilerParams(
-            collective_id=1, has_side_effects=True, vmem_limit_bytes=60 * MIB
+            collective_id=0, has_side_effects=True, vmem_limit_bytes=60 * MIB
         ),
-        name="step",
-    )(part, wide, energy_row)
+        name="site",
+    )(wave, row_ops, col_ops, count, source, target, energy_row)
 
 
 def renorm_kernel(count, source, target, src_block, tgt_block, cols, root, level, exact, energy, out, wave_o, energy_o):
@@ -670,13 +652,9 @@
 
 
 def on_device(wave_in, row_energy, row_operators, column_operators, term_count, source, target):
-    wide, row_sib, col_sib, table_sib = gather(
-        wave_in, row_operators, column_operators, term_count, source, target
+    stepped, root, level, exact, energy = site(
+        wave_in, row_operators, column_operators, term_count, source, target, row_energy.reshape(8, 128)
     )
-    part = terms(
-        term_count, source, target, table_sib, row_operators, row_sib, column_operators, col_sib, wide
-    )
-    stepped, root, level, exact, energy = step(part, wide, row_energy.reshape(8, 128))
     renormalized, wave_next, energy = renorm(
         term_count, source, target, stepped, column_operators, root, level, exact, energy
     )

time: 133 us -> 124 us (0.932)
  the two profiles are of different devices: /device:TPU:20 before, /device:TPU:1 now
where the time goes in v2:
time: 124 us; the launch traced here: 122 us
  Pallas kernels  121 us (98%)
  between operations  1.29 us (1%)
    pallas_call x1, Pallas kernels, site(): pl.pallas_call(site_kernel, out_shape=(jax.ShapeDtypeStruct((2, CHIPS, SE...  109 us
    pallas_call x1, Pallas kernels, renorm(): pl.pallas_call(renorm_kernel, out_shape=(jax.ShapeDtypeStruct((4, 2 * SEC...  12.2 us

profile of v2, /device:TPU:1, one launch (start us, length us, event | category | flops | bytes accessed | tf_op | source)
XLA Modules:
  0.0 122.1 jit_solution(16777096112670918076)
XLA Ops:
  1.3 108.6 %site.1 = (bf16[2,16,512,256]{3,2,1,0:T(8,128)(2,1)}, bf16[2,512,512]{2,1,0:T(8,128)(2,1)}, f32[2,8,128]{2,1,0:T(8,128)}, f32[1024,128]{1,0:T(8,128)}, f32[8,128]{1,0:T(8,128)}) custom-call(bf16[1024,128]{1,0:T(8,128)(2,1)} %wave.1, bf16[4,1024,512]{2,1,0:T(8,128)(2,1)} %row_ops.1, bf16[4,512,512]{2,1,0:T(8,128)(2,1)} %cols.1, s32[1]{0:T(128)S(6)} %copy.10.count, ...), custom_call_target="tpu_custom_call" | custom-call | tf_op jit(solution)/shard_map/site/pallas_call | solution.py:509
  109.9 12.2 %renorm.1 = (f32[4,1024,512]{2,1,0:T(8,128)}, f32[1024,128]{1,0:T(8,128)}, f32[1]{0:T(128)}) custom-call(s32[1]{0:T(128)S(6)} %copy.10.count, s32[4]{0:T(128)} %source.3, s32[4]{0:T(128)} %target.3, bf16[2,16,512,256]{3,2,1,0:T(8,128)(2,1)} %get-tuple-element.11.src_block.tgt_block, bf16[2,16,512,256]{3,2,1,0:T(8,128)(2,1)} %get-tuple-element.11.src_block.tgt_block, ...), custom_call_target="tpu_custom_call" | custom-call | tf_op jit(solution)/shard_map/renorm/pallas_call | solution.py:624

commit v3 on v2

--- a/solution.py
+++ b/solution.py
@@ -15,6 +15,7 @@
 WIDE = 256
 HALF = 256
 QUARTER = 128
+EIGHTH = 64
 MIB = 1 << 20
 MESH = pl.DeviceIdType.MESH
 OPS = ("x", "z", "core")
@@ -83,10 +84,13 @@
         left, right = turn(p, -1), turn(p, 1)
         arrived(h, 0, left, q, None)
         go(h, 2, left, q, 0, 0, 1)
+        arrived(h, 1, right, q, None)
+        go(h, 3, right, q, 1, 0, -1)
+    for h in (0, 1):
+        p, q = places[h]
+        left, right = turn(p, -1), turn(p, 1)
         go(h, 5, left, q, None, 1, 1)
         go(h, 9, left, q, None, 1, -1)
-        arrived(h, 1, right, q, None)
-        go(h, 3, right, q, 1, 0, -1)
         go(h, 6, right, q, None, 1, 1)
         go(h, 10, right, q, None, 1, -1)
     yield
@@ -151,107 +155,129 @@
     return dot(a.astype(BF16), b.astype(BF16))
 
 
-def reduce_blocks(part, near, whole, near2, whole2, total, x, z, send, recv, send2, recv2):
-    names = (("z", "x"), ("x", "z"))
-    places = ((z, x), (x, z))
-
-    def block(h, pa, pb):
-        return pb * 4 + pa if h == 0 else pa * 4 + pb
-
-    def rows(h, half):
-        return pl.ds(h * HALF + half * QUARTER, QUARTER)
-
-    def local(half):
-        return pl.ds(half * QUARTER, QUARTER)
-
-    def order(h):
-        q = places[h][1]
+class Reduction:
+    def __init__(self, bufs, sems, x, z):
+        self.part, self.near, self.whole, self.near2, self.whole2, self.total = bufs
+        self.send, self.recv, self.mod_send, self.mod_recv, self.send2, self.recv2 = sems
+        self.places = ((z, x), (x, z))
+        self.sent = []
+
+    def at(self, h, pa, pb):
+        return (pb, pa) if h == 0 else (pa, pb)
+
+    def rows(self, w, h, half):
+        return pl.ds(w * HALF + h * QUARTER + half * EIGHTH, EIGHTH)
+
+    def both_rows(self, w, h):
+        return pl.ds(w * HALF + h * QUARTER, QUARTER)
+
+    def line(self, w, h, pa, half):
+        rows = self.rows(w, h, half)
+        return self.part.at[:, pa, rows, :] if h == 0 else self.part.at[pa, :, rows, :]
+
+    def order(self, h):
+        q = self.places[h][1]
         return (turn(q, 2), turn(q, 1), turn(q, -1), q)
 
-    sent = []
-
-    def go(one):
+    def peer(self, h, axis, d):
+        return {("zx", "xz")[h][axis]: turn(self.places[h][axis], 1 - 2 * d)}
+
+    def go(self, one):
         one.start()
-        sent.append(one)
-
-    def near_copy(h, d, i):
-        p = places[h][0]
-        src = part.at[block(h, turn(p, 2), order(h)[i]), rows(h, d), :]
-        to = {names[h][0]: turn(p, 1 - 2 * d)}
-        return push(src, near.at[h, d, i], send.at[h, d, i], recv.at[h, d, i], to)
-
-    def whole_copy(h, d, i, half):
-        p = places[h][0]
-        src = part.at[block(h, turn(p, 1 - 2 * d), order(h)[i]), rows(h, half), :]
-        to = {names[h][0]: turn(p, 1 - 2 * d)}
+        self.sent.append(one)
+
+    def near_copy(self, w, h, d):
+        src = self.line(w, h, turn(self.places[h][0], 2), d)
+        return push(src, self.near.at[w, h, d], self.send.at[w, h, d], self.recv.at[w, h, d], self.peer(h, 0, d))
+
+    def plain_copy(self, w, h, d):
+        src = self.line(w, h, turn(self.places[h][0], 1 - 2 * d), 1 - d)
+        dst = self.whole.at[w, h, d, :, pl.ds((1 - d) * EIGHTH, EIGHTH), :]
+        return push(src, dst, self.send.at[w, h, 2 + d], self.recv.at[w, h, 2 + d], self.peer(h, 0, d))
+
+    def added_copy(self, w, h, d, i):
+        to = self.order(h)[i]
+        src = self.part.at[*self.at(h, turn(self.places[h][0], 1 - 2 * d), to), self.rows(w, h, d), :]
+        dst = self.whole.at[w, h, d, to, pl.ds(d * EIGHTH, EIGHTH), :]
+        return push(src, dst, self.mod_send.at[w, h, d, i], self.mod_recv.at[w, h, d, i], self.peer(h, 0, d))
+
+    def near2_copy(self, w, h, d):
+        p, q = self.places[h]
+        src = self.part.at[*self.at(h, p, turn(q, 2)), self.rows(w, h, d), :]
+        return push(src, self.near2.at[w, h, d], self.send2.at[w, h, d], self.recv2.at[w, h, d], self.peer(h, 1, d))
+
+    def whole2_copy(self, w, h, d, half):
+        p, q = self.places[h]
         j = 2 + 2 * d + half
-        return push(src, whole.at[h, d, i, local(half), :], send.at[h, j, i], recv.at[h, j, i], to)
-
-    def near2_copy(h, d):
-        p, q = places[h]
-        src = part.at[block(h, p, turn(q, 2)), rows(h, d), :]
-        return push(src, near2.at[h, d], send2.at[h, d], recv2.at[h, d], {names[h][1]: turn(q, 1 - 2 * d)})
-
-    def whole2_copy(h, d, half):
-        p, q = places[h]
-        j = 2 + 2 * d + half
-        src = part.at[block(h, p, turn(q, 1 - 2 * d)), rows(h, half), :]
-        to = {names[h][1]: turn(q, 1 - 2 * d)}
-        return push(src, whole2.at[h, d, local(half), :], send2.at[h, j], recv2.at[h, j], to)
-
-    for i in range(4):
+        src = self.part.at[*self.at(h, p, turn(q, 1 - 2 * d)), self.rows(w, h, half), :]
+        dst = self.whole2.at[w, h, d, pl.ds(half * EIGHTH, EIGHTH), :]
+        return push(src, dst, self.send2.at[w, h, j], self.recv2.at[w, h, j], self.peer(h, 1, d))
+
+    def begin(self, w):
         for h in (0, 1):
             for d in (0, 1):
-                go(near_copy(h, d, i))
-    for i in range(4):
+                self.go(self.near_copy(w, h, d))
         for h in (0, 1):
             for d in (0, 1):
-                go(whole_copy(h, d, i, 1 - d))
-    for i in range(4):
+                self.go(self.plain_copy(w, h, d))
+
+    def add(self, w):
         for h in (0, 1):
-            p = places[h][0]
+            p = self.places[h][0]
             for d in (0, 1):
-                near_copy(h, d, i).wait_recv()
-                at = block(h, turn(p, 1 - 2 * d), order(h)[i])
-                both = part[at, rows(h, d), :].astype(F32) + near[h, d, i].astype(F32)
-                part[at, rows(h, d), :] = both.astype(BF16)
-                go(whole_copy(h, d, i, d))
-    for i in range(4):
+                self.near_copy(w, h, d).wait_recv()
+                for i in range(4):
+                    to = self.order(h)[i]
+                    spot = (*self.at(h, turn(p, 1 - 2 * d), to), self.rows(w, h, d), slice(None))
+                    both = self.part[spot].astype(F32) + self.near[w, h, d, to].astype(F32)
+                    self.part[spot] = both.astype(BF16)
+                    self.go(self.added_copy(w, h, d, i))
+
+    def second(self, w):
         for h in (0, 1):
-            p, q = places[h]
+            for d in (0, 1):
+                self.plain_copy(w, h, d).wait_recv()
+        for i in range(4):
+            for h in (0, 1):
+                p = self.places[h][0]
+                for d in (0, 1):
+                    self.added_copy(w, h, d, i).wait_recv()
+                to = self.order(h)[i]
+                spot = (*self.at(h, p, to), self.both_rows(w, h), slice(None))
+                done = self.part[spot].astype(F32) + self.whole[w, h, 0, to].astype(F32) + self.whole[w, h, 1, to].astype(F32)
+                if i == 3:
+                    self.total[self.both_rows(w, h), :] = done
+                else:
+                    self.part[spot] = done.astype(BF16)
+                if i == 0:
+                    self.go(self.near2_copy(w, h, 0))
+                    self.go(self.near2_copy(w, h, 1))
+                if i == 1:
+                    self.go(self.whole2_copy(w, h, 0, 1))
+                if i == 2:
+                    self.go(self.whole2_copy(w, h, 1, 0))
+
+    def add2(self, w):
+        for h in (0, 1):
+            p, q = self.places[h]
+            for d in (0, 1):
+                self.near2_copy(w, h, d).wait_recv()
+                spot = (*self.at(h, p, turn(q, 1 - 2 * d)), self.rows(w, h, d), slice(None))
+                both = self.part[spot].astype(F32) + self.near2[w, h, d].astype(F32)
+                self.part[spot] = both.astype(BF16)
+                self.go(self.whole2_copy(w, h, d, d))
+
+    def finish(self, w):
+        for h in (0, 1):
             for d in (0, 1):
                 for half in (0, 1):
-                    whole_copy(h, d, i, half).wait_recv()
-            at = block(h, p, order(h)[i])
-            here = pl.ds(h * HALF, HALF)
-            done = part[at, here, :].astype(F32) + whole[h, 0, i].astype(F32) + whole[h, 1, i].astype(F32)
-            if i == 3:
-                total[here, :] = done
-            else:
-                part[at, here, :] = done.astype(BF16)
-            if i == 0:
-                go(near2_copy(h, 0))
-                go(near2_copy(h, 1))
-            if i == 1:
-                go(whole2_copy(h, 0, 1))
-            if i == 2:
-                go(whole2_copy(h, 1, 0))
-    for h in (0, 1):
-        p, q = places[h]
-        for d in (0, 1):
-            near2_copy(h, d).wait_recv()
-            at = block(h, p, turn(q, 1 - 2 * d))
-            both = part[at, rows(h, d), :].astype(F32) + near2[h, d].astype(F32)
-            part[at, rows(h, d), :] = both.astype(BF16)
-            go(whole2_copy(h, d, d))
-    for h in (0, 1):
-        for d in (0, 1):
-            for half in (0, 1):
-                whole2_copy(h, d, half).wait_recv()
-        here = pl.ds(h * HALF, HALF)
-        total[here, :] += whole2[h, 0].astype(F32) + whole2[h, 1].astype(F32)
-    for one in sent:
-        one.wait_send()
+                    self.whole2_copy(w, h, d, half).wait_recv()
+            here = self.both_rows(w, h)
+            self.total[here, :] += self.whole2[w, h, 0].astype(F32) + self.whole2[w, h, 1].astype(F32)
+
+    def close(self):
+        for one in self.sent:
+            one.wait_send()
 
 
 def frobenius(a):
@@ -282,7 +308,7 @@
     wide, row_v, col_v, table, table_in, table_s, order_s, source_s, prefix,
     part, near, whole, near2, whole2, total, summed, stepped, gram, my, mm, mu, mz, roots, level_two, exact, scalars, energy_col,
     wv_send, wv_recv, swap_send, swap_recv,
-    rs_send, rs_recv, rs2_send, rs2_recv, ag_send, ag_recv, en_send, en_recv, st_send, st_recv, st_own,
+    rs_send, rs_recv, mod_send, mod_recv, rs2_send, rs2_recv, ag_send, ag_recv, en_send, en_recv, st_send, st_recv, st_own,
     end_send, end_recv, own_sem,
 ):
     x, z, c, y = lax.axis_index("x"), lax.axis_index("z"), lax.axis_index("core"), lax.axis_index("sec")
@@ -360,6 +386,9 @@
     swaps[2].wait()
     swaps[3].wait()
 
+    reduction = Reduction(
+        (part, near, whole, near2, whole2, total), (rs_send, rs_recv, mod_send, mod_recv, rs2_send, rs2_recv), x, z
+    )
     prefix[0] = jnp.zeros((HALF, SEC), F32)
     for h in (0, 1):
         here = pl.ds(h * HALF, HALF)
@@ -376,10 +405,14 @@
         lax.fori_loop(0, 8, term, 0)
         for t in range(8):
             added = (prefix[starts[t + 1]] - prefix[starts[t]]).astype(BF16)
-            part[2 * t, here, :] = added[:, :WIDE]
-            part[2 * t + 1, here, :] = added[:, WIDE:]
-
-    reduce_blocks(part, near, whole, near2, whole2, total, x, z, rs_send, rs_recv, rs2_send, rs2_recv)
+            part[t // 2, 2 * (t % 2), here, :] = added[:, :WIDE]
+            part[t // 2, 2 * (t % 2) + 1, here, :] = added[:, WIDE:]
+        reduction.begin(h)
+
+    for work in (reduction.add, reduction.second, reduction.add2, reduction.finish):
+        work(0)
+        work(1)
+    reduction.close()
     summed[b] = total[...].astype(BF16)
     steps = all_blocks(summed, x, z, ag_send, ag_recv)
     next(steps)
@@ -527,11 +560,11 @@
             pltpu.SMEM((8,), jnp.int32),
             pltpu.SMEM((8,), jnp.int32),
             pltpu.VMEM((9, HALF, SEC), F32),
-            blocks,
-            pltpu.VMEM((2, 2, 4, QUARTER, WIDE), BF16),
-            pltpu.VMEM((2, 2, 4, HALF, WIDE), BF16),
-            pltpu.VMEM((2, 2, QUARTER, WIDE), BF16),
-            pltpu.VMEM((2, 2, HALF, WIDE), BF16),
+            pltpu.VMEM((4, 4, SEC, WIDE), BF16),
+            pltpu.VMEM((2, 2, 2, 4, EIGHTH, WIDE), BF16),
+            pltpu.VMEM((2, 2, 2, 4, QUARTER, WIDE), BF16),
+            pltpu.VMEM((2, 2, 2, EIGHTH, WIDE), BF16),
+            pltpu.VMEM((2, 2, 2, QUARTER, WIDE), BF16),
             pltpu.VMEM((SEC, WIDE), F32),
             blocks,
             blocks,
@@ -549,10 +582,12 @@
             dma((2, 20)),
             dma((4,)),
             dma((4,)),
-            dma((2, 6, 4)),
-            dma((2, 6, 4)),
-            dma((2, 6)),
-            dma((2, 6)),
+            dma((2, 2, 4)),
+            dma((2, 2, 4)),
+            dma((2, 2, 2, 4)),
+            dma((2, 2, 2, 4)),
+            dma((2, 2, 6)),
+            dma((2, 2, 6)),
             dma((2, 20)),
             dma((2, 20)),
             dma((4, 4)),
@@ -571,56 +606,92 @@
     )(wave, row_ops, col_ops, count, source, target, energy_row)
 
 
-def renorm_kernel(count, source, target, src_block, tgt_block, cols, root, level, exact, energy, out, wave_o, energy_o):
-    k = pl.program_id(0)
-    scale = level[0, 0:1, 0:1]
-
-    @pl.when(k == 0)
-    def first():
-        energy_o[0] = energy[0, 0]
-        wave_o[...] = scale * exact[...] + dot(root[0], exact[...].astype(BF16))
-
-    @pl.when(k < count[0])
-    def live():
-        product = None
-        for part in (0, 1):
-            block = src_block[0, part]
-            half = (scale * block.astype(F32) + dot(root[0], block)).astype(BF16)
-            added = dot(half, cols[0, part * WIDE : (part + 1) * WIDE, :])
-            product = added if product is None else product + added
-        product = product.astype(BF16)
-        total = None
-        for part in (0, 1):
-            block = tgt_block[0, part]
-            half = (scale * block.astype(F32) + dot(root[0], block)).astype(BF16)
-            added = dot_t(product[:, part * WIDE : (part + 1) * WIDE], half)
-            total = added if total is None else total + added
-        out[0] = total * SEC ** (-0.5)
-
-    @pl.when(k >= count[0])
-    def empty():
-        out[...] = jnp.zeros_like(out)
+def renorm_kernel(
+    count, source, target, stepped, cols, root, level, exact, energy,
+    out, wave_o, energy_o,
+    block_v, cols_v, root_v, out_v, zero_v, exact_v, wave_v, block_sem, cols_sem, root_sem, out_sem, exact_sem, wave_sem,
+):
+    energy_o[0] = energy[0, 0]
+
+    def needs(k, s):
+        pair = (source[k], target[k])
+        return [
+            pltpu.make_async_copy(
+                stepped.at[s, pl.ds(2 * pair[e], 2)], block_v.at[k, s, e], block_sem.at[k, s, e]
+            )
+            for e in (0, 1)
+        ]
+
+    def column_op(k):
+        return pltpu.make_async_copy(cols.at[k], cols_v.at[k], cols_sem.at[k])
+
+    def result(k, s):
+        return pltpu.make_async_copy(out_v.at[k, s], out.at[k, pl.ds(s * SEC, SEC), :], out_sem.at[k, s])
+
+    def nothing(k, s):
+        return pltpu.make_async_copy(zero_v, out.at[k, pl.ds(s * SEC, SEC), :], out_sem.at[k, s])
+
+    roots = [pltpu.make_async_copy(root.at[s], root_v.at[s], root_sem.at[s]) for s in (0, 1)]
+    roots[0].start()
+    for k in range(4):
+
+        @pl.when(k < count[0])
+        def fetch(k=k):
+            column_op(k).start()
+            for s in (0, 1):
+                for one in needs(k, s):
+                    one.start()
+
+        if k == 0:
+            roots[1].start()
+    zero_v[...] = jnp.zeros_like(zero_v)
+    for k in range(1, 4):
+
+        @pl.when(k >= count[0])
+        def clear(k=k):
+            nothing(k, 0).start()
+            nothing(k, 1).start()
+
+    load_exact = pltpu.make_async_copy(exact, exact_v, exact_sem)
+    load_exact.start()
+    for one in roots:
+        one.wait()
+
+    def one_term(k, carry):
+        column_op(k).wait()
+        for s in (0, 1):
+            scale = level[s, 0:1, 0:1]
+            for one in needs(k, s):
+                one.wait()
+            halves = []
+            for e in (0, 1):
+                block = jnp.concatenate([block_v[k, s, e, 0], block_v[k, s, e, 1]], axis=1)
+                halves.append((scale * block.astype(F32) + dot(root_v[s], block)).astype(BF16))
+            product = dot(halves[0], cols_v[k]).astype(BF16)
+            out_v[k, s] = dot_t(product, halves[1]) * SEC ** (-0.5)
+            result(k, s).start()
+        return carry
+
+    lax.fori_loop(0, count[0], one_term, 0)
+    load_exact.wait()
+    waves = []
+    for s in (0, 1):
+        rows = pl.ds(s * SEC, SEC)
+        own = exact_v[rows, :]
+        wave_v[rows, :] = level[s, 0:1, 0:1] * own + dot(root_v[s], own.astype(BF16))
+        waves.append(pltpu.make_async_copy(wave_v.at[rows, :], wave_o.at[rows, :], wave_sem.at[s]))
+        waves[s].start()
+    for one in waves:
+        one.wait()
+    for k in range(4):
+        for s in (0, 1):
+            result(k, s).wait()
 
 
 def renorm(count, source, target, stepped, cols, root, level, exact, energy):
-    def slot(k, count):
-        return jnp.minimum(k, count[0] - 1)
-
-    def sector(k, s, count):
-        return jnp.where(k < count[0], s, 1)
-
-    def src_at(k, s, count, source, target):
-        return (sector(k, s, count), source[slot(k, count)], 0, 0)
-
-    def tgt_at(k, s, count, source, target):
-        return (sector(k, s, count), target[slot(k, count)], 0, 0)
-
-    def root_at(k, s, count, source, target):
-        return (sector(k, s, count), 0, 0)
-
-    def once_at(k, s, count, source, target):
-        return (jnp.where(k == 0, s, 1), 0)
-
+    hbm = pl.BlockSpec(memory_space=pltpu.HBM)
+    vmem = pl.BlockSpec(memory_space=pltpu.VMEM)
+    smem = pl.BlockSpec(memory_space=pltpu.SMEM)
     return pl.pallas_call(
         renorm_kernel,
         out_shape=(
@@ -628,27 +699,26 @@
             jax.ShapeDtypeStruct((2 * SEC, 128), F32),
             jax.ShapeDtypeStruct((1,), F32),
         ),
-        grid_spec=pltpu.PrefetchScalarGridSpec(
-            num_scalar_prefetch=3,
-            grid=(4, 2),
-            in_specs=[
-                pl.BlockSpec((1, 2, SEC, WIDE), src_at),
-                pl.BlockSpec((1, 2, SEC, WIDE), tgt_at),
-                pl.BlockSpec((1, SEC, SEC), lambda k, s, count, source, target: (slot(k, count), 0, 0)),
-                pl.BlockSpec((1, SEC, SEC), root_at),
-                pl.BlockSpec((1, 8, 128), root_at),
-                pl.BlockSpec((SEC, 128), once_at),
-                pl.BlockSpec(memory_space=pltpu.SMEM),
-            ],
-            out_specs=[
-                pl.BlockSpec((1, SEC, SEC), lambda k, s, count, source, target: (k, s, 0)),
-                pl.BlockSpec((SEC, 128), once_at),
-                pl.BlockSpec(memory_space=pltpu.SMEM),
-            ],
-        ),
+        in_specs=[smem] * 3 + [hbm] * 3 + [vmem, hbm, smem],
+        out_specs=(hbm, hbm, smem),
+        scratch_shapes=[
+            pltpu.VMEM((4, 2, 2, 2, SEC, WIDE), BF16),
+            pltpu.VMEM((4, SEC, SEC), BF16),
+            pltpu.VMEM((2, SEC, SEC), BF16),
+            pltpu.VMEM((4, 2, SEC, SEC), F32),
+            pltpu.VMEM((SEC, SEC), F32),
+            pltpu.VMEM((2 * SEC, 128), F32),
+            pltpu.VMEM((2 * SEC, 128), F32),
+            pltpu.SemaphoreType.DMA((4, 2, 2)),
+            pltpu.SemaphoreType.DMA((4,)),
+            pltpu.SemaphoreType.DMA((2,)),
+            pltpu.SemaphoreType.DMA((4, 2)),
+            pltpu.SemaphoreType.DMA(()),
+            pltpu.SemaphoreType.DMA((2,)),
+        ],
         compiler_params=pltpu.CompilerParams(vmem_limit_bytes=60 * MIB),
         name="renorm",
-    )(count, source, target, stepped, stepped, cols, root, level, exact, energy)
+    )(count, source, target, stepped, cols, root, level, exact, energy)
 
 
 def on_device(wave_in, row_energy, row_operators, column_operators, term_count, source, target):

time: 124 us -> 118 us (0.952)
  the two profiles are of different devices: /device:TPU:1 before, /device:TPU:0 now
where the time goes in v3:
time: 118 us
  Pallas kernels  117 us (99%)
  between operations  1.29 us (1%)
    pallas_call x1, Pallas kernels, site(): pl.pallas_call(site_kernel, out_shape=(jax.ShapeDtypeStruct((2, CHIPS, SE...  102 us
    pallas_call x1, Pallas kernels, renorm(): pl.pallas_call(renorm_kernel, out_shape=(jax.ShapeDtypeStruct((4, 2 * SEC...  14.8 us

profile of v3, /device:TPU:0, one launch (start us, length us, event | category | flops | bytes accessed | tf_op | source)
XLA Modules:
  0.0 117.9 jit_solution(15986108434334691712)
XLA Ops:
  1.3 101.8 %site.1 = (bf16[2,16,512,256]{3,2,1,0:T(8,128)(2,1)}, bf16[2,512,512]{2,1,0:T(8,128)(2,1)}, f32[2,8,128]{2,1,0:T(8,128)}, f32[1024,128]{1,0:T(8,128)}, f32[8,128]{1,0:T(8,128)}) custom-call(bf16[1024,128]{1,0:T(8,128)(2,1)} %wave.1, bf16[4,1024,512]{2,1,0:T(8,128)(2,1)} %row_ops.1, bf16[4,512,512]{2,1,0:T(8,128)(2,1)} %cols.1, s32[1]{0:T(128)S(6)} %copy.10.count, ...), custom_call_target="tpu_custom_call" | custom-call | tf_op jit(solution)/shard_map/site/pallas_call | solution.py:542
  103.1 14.8 %renorm.1 = (f32[4,1024,512]{2,1,0:T(8,128)}, f32[1024,128]{1,0:T(8,128)}, f32[1]{0:T(128)}) custom-call(s32[1]{0:T(128)S(6)} %copy.10.count, s32[4]{0:T(128)} %source.3, s32[4]{0:T(128)} %target.3, bf16[2,16,512,256]{3,2,1,0:T(8,128)(2,1)} %get-tuple-element.11.stepped, bf16[4,512,512]{2,1,0:T(8,128)(2,1)} %cols.1, ...), custom_call_target="tpu_custom_call" | custom-call | tf_op jit(solution)/shard_map/renorm/pallas_call | solution.py:695

commit v4 on v3

--- a/solution.py
+++ b/solution.py
@@ -16,6 +16,7 @@
 HALF = 256
 QUARTER = 128
 EIGHTH = 64
+CUT = (3,)
 MIB = 1 << 20
 MESH = pl.DeviceIdType.MESH
 OPS = ("x", "z", "core")
@@ -40,19 +41,17 @@
     pl.semaphore_wait(barrier, len(peers))
 
 
-def all_blocks(buf, x, z, send, recv):
+def all_blocks(buf, x, z, send, recv, late=None, cut=(), apart=False):
     names = (("x", "z"), ("z", "x"))
     places = ((x, z), (z, x))
+    every = slice(None)
 
     def block(h, pa, pb):
         return pa * 4 + pb if h == 0 else pb * 4 + pa
 
-    def view(h, pa, pb, part):
+    def copy(h, j, pa, pb, part, axis, by, columns=every):
         rows = pl.ds(h * HALF, HALF) if part is None else pl.ds(h * HALF + part * QUARTER, QUARTER)
-        return buf.at[block(h, pa, pb), rows, :]
-
-    def copy(h, j, pa, pb, part, axis, by):
-        ref = view(h, pa, pb, part)
+        ref = buf.at[block(h, pa, pb), rows, columns]
         to = {names[h][axis]: turn(places[h][axis], by)}
         return push(ref, ref, send.at[h, j], recv.at[h, j], to)
 
@@ -67,69 +66,99 @@
         one.start()
         sent.append(one)
 
-    def arrived(h, j, pa, pb, part):
-        copy(h, j, pa, pb, part, 0, 1).wait_recv()
-
-    for h in (0, 1):
-        p, q = places[h]
-        go(h, 0, p, q, None, 0, 1)
-        go(h, 1, p, q, None, 0, -1)
-    for h in (0, 1):
-        p, q = places[h]
-        go(h, 4, p, q, None, 1, 1)
-        go(h, 8, p, q, None, 1, -1)
-    yield
-    for h in (0, 1):
-        p, q = places[h]
-        left, right = turn(p, -1), turn(p, 1)
-        arrived(h, 0, left, q, None)
-        go(h, 2, left, q, 0, 0, 1)
-        arrived(h, 1, right, q, None)
-        go(h, 3, right, q, 1, 0, -1)
-    for h in (0, 1):
-        p, q = places[h]
-        left, right = turn(p, -1), turn(p, 1)
-        go(h, 5, left, q, None, 1, 1)
-        go(h, 9, left, q, None, 1, -1)
-        go(h, 6, right, q, None, 1, 1)
-        go(h, 10, right, q, None, 1, -1)
-    yield
+    def arrived(h, j, pa, pb, part, columns=every):
+        copy(h, j, pa, pb, part, 0, 1, columns).wait_recv()
+
+    def across(h, i):
+        pa, q = order(h)[i], places[h][1]
+        for d in (0, 1):
+            for n in (0, 1) if i in cut else (0,):
+                part = (d + n) % 2 if i in cut else None
+                go(h, 8 + 4 * i + 2 * d + n, pa, q, part, 1, 1 - 2 * d)
+
+    def across_arrived(h, i, d, n):
+        part = (d + n) % 2 if i in cut else None
+        arrived(h, 8 + 4 * i + 2 * d + n, order(h)[i], turn(places[h][1], 2 * d - 1), part)
 
     def onward(h, i):
         pa, q = order(h)[i], places[h][1]
-        arrived(h, 4 + i, pa, turn(q, -1), None)
-        go(h, 12 + i, pa, turn(q, -1), 0, 1, 1)
-        arrived(h, 8 + i, pa, turn(q, 1), None)
-        go(h, 16 + i, pa, turn(q, 1), 1, 1, -1)
-
+        for d in (0, 1):
+            across_arrived(h, i, d, 0)
+            go(h, 24 + 2 * i + d, pa, turn(q, 2 * d - 1), d, 1, 1 - 2 * d)
+
+    def rest(h, i):
+        if i in cut:
+            across_arrived(h, i, 0, 1)
+            across_arrived(h, i, 1, 1)
+
+    def first(h, columns, j):
+        p, q = places[h]
+        go(h, j, p, q, None, 0, 1, columns)
+        go(h, j + 1, p, q, None, 0, -1, columns)
+
+    if late is None:
+        for h in (0, 1):
+            first(h, every, 0)
+            if apart:
+                across(h, 0)
+                yield
+    else:
+        for h in (0, 1):
+            first(h, late[0], 0)
+        late[2]()
+        for h in (0, 1):
+            first(h, late[1], 2)
+    if not apart:
+        for h in (0, 1):
+            across(h, 0)
+        yield
+    for h in (0, 1):
+        p, q = places[h]
+        for d in (0, 1):
+            side = turn(p, 2 * d - 1)
+            if late is None:
+                arrived(h, d, side, q, None)
+            else:
+                arrived(h, d, side, q, None, late[0])
+                arrived(h, 2 + d, side, q, None, late[1])
+            go(h, 4 + d, side, q, d, 0, 1 - 2 * d)
+    for h in (0, 1):
+        across(h, 1)
+        across(h, 2)
+    yield
     for h in (0, 1):
         onward(h, 0)
+    for h in (0, 1):
+        rest(h, 0)
     yield 1
     for h in (0, 1):
         p, q = places[h]
-        far = turn(p, 2)
-        arrived(h, 2, far, q, 0)
-        arrived(h, 3, far, q, 1)
-        go(h, 7, far, q, None, 1, 1)
-        go(h, 11, far, q, None, 1, -1)
+        arrived(h, 4, turn(p, 2), q, 0)
+        arrived(h, 5, turn(p, 2), q, 1)
+        across(h, 3)
     yield
     for h in (0, 1):
         onward(h, 1)
     yield
     for h in (0, 1):
         onward(h, 2)
+    for h in (0, 1):
+        rest(h, 1)
+        rest(h, 2)
     yield 2
 
     def last(i):
         for h in (0, 1):
             pa, far = order(h)[i], turn(places[h][1], 2)
-            arrived(h, 12 + i, pa, far, 0)
-            arrived(h, 16 + i, pa, far, 1)
+            arrived(h, 24 + 2 * i, pa, far, 0)
+            arrived(h, 25 + 2 * i, pa, far, 1)
 
     last(0)
     yield 3
     for h in (0, 1):
         onward(h, 3)
+    for h in (0, 1):
+        rest(h, 3)
     last(1)
     last(2)
     yield 4
@@ -339,8 +368,11 @@
     ]
     swaps[0].start()
     own_wave.wait()
-    push(wave.at[other, :], wide.at[b, :, other_columns], swap_send.at[0], swap_recv.at[0], sib).wait_recv()
-    steps = all_blocks(wide, x, z, wv_send, wv_recv)
+
+    def swapped():
+        push(wave.at[other, :], wide.at[b, :, other_columns], swap_send.at[0], swap_recv.at[0], sib).wait_recv()
+
+    steps = all_blocks(wide, x, z, wv_send, wv_recv, (columns, other_columns, swapped), CUT)
     next(steps)
     for swap in swaps[1:]:
         swap.start()
@@ -409,13 +441,16 @@
             part[t // 2, 2 * (t % 2) + 1, here, :] = added[:, WIDE:]
         reduction.begin(h)
 
-    for work in (reduction.add, reduction.second, reduction.add2, reduction.finish):
+    for work in (reduction.add, reduction.second, reduction.add2):
         work(0)
         work(1)
+    steps = all_blocks(summed, x, z, ag_send, ag_recv, None, CUT, True)
+    for h in (0, 1):
+        reduction.finish(h)
+        here = pl.ds(h * HALF, HALF)
+        summed[b, here, :] = total[here, :].astype(BF16)
+        next(steps)
     reduction.close()
-    summed[b] = total[...].astype(BF16)
-    steps = all_blocks(summed, x, z, ag_send, ag_recv)
-    next(steps)
     level = energy_col[...]
     amplitude = wide[b].astype(F32)
     applied = level * amplitude + total[...]
@@ -578,8 +613,8 @@
             pltpu.VMEM((2, SEC, 128), F32),
             pltpu.VMEM((4, 4, 8, 128), F32),
             pltpu.VMEM((SEC, 1), F32),
-            dma((2, 20)),
-            dma((2, 20)),
+            dma((2, 32)),
+            dma((2, 32)),
             dma((4,)),
             dma((4,)),
             dma((2, 2, 4)),
@@ -588,8 +623,8 @@
             dma((2, 2, 2, 4)),
             dma((2, 2, 6)),
             dma((2, 2, 6)),
-            dma((2, 20)),
-            dma((2, 20)),
+            dma((2, 32)),
+            dma((2, 32)),
             dma((4, 4)),
             dma((4, 4)),
             dma((CHIPS,)),
@@ -609,7 +644,7 @@
 def renorm_kernel(
     count, source, target, stepped, cols, root, level, exact, energy,
     out, wave_o, energy_o,
-    block_v, cols_v, root_v, out_v, zero_v, exact_v, wave_v, block_sem, cols_sem, root_sem, out_sem, exact_sem, wave_sem,
+    block_v, cols_v, root_v, out_v, zero_v, exact_v, wave_v, level_v, block_sem, cols_sem, root_sem, out_sem, exact_sem, wave_sem, level_sem,
 ):
     energy_o[0] = energy[0, 0]
 
@@ -632,37 +667,49 @@
         return pltpu.make_async_copy(zero_v, out.at[k, pl.ds(s * SEC, SEC), :], out_sem.at[k, s])
 
     roots = [pltpu.make_async_copy(root.at[s], root_v.at[s], root_sem.at[s]) for s in (0, 1)]
+    load_level = pltpu.make_async_copy(level, level_v, level_sem)
+    load_level.start()
     roots[0].start()
-    for k in range(4):
-
-        @pl.when(k < count[0])
-        def fetch(k=k):
-            column_op(k).start()
-            for s in (0, 1):
-                for one in needs(k, s):
-                    one.start()
-
-        if k == 0:
-            roots[1].start()
+    for one in needs(0, 0):
+        one.start()
+    column_op(0).start()
+    roots[1].start()
+    for one in needs(0, 1):
+        one.start()
     zero_v[...] = jnp.zeros_like(zero_v)
-    for k in range(1, 4):
-
-        @pl.when(k >= count[0])
-        def clear(k=k):
-            nothing(k, 0).start()
-            nothing(k, 1).start()
-
     load_exact = pltpu.make_async_copy(exact, exact_v, exact_sem)
-    load_exact.start()
-    for one in roots:
-        one.wait()
+    load_level.wait()
+    roots[0].wait()
 
     def one_term(k, carry):
         column_op(k).wait()
         for s in (0, 1):
-            scale = level[s, 0:1, 0:1]
+            scale = level_v[s, 0:1, 0:1]
             for one in needs(k, s):
                 one.wait()
+            if s == 0:
+
+                @pl.when(k + 1 < count[0])
+                def ahead():
+                    column_op(k + 1).start()
+                    for t in (0, 1):
+                        for one in needs(k + 1, t):
+                            one.start()
+
+                @pl.when(k == 0)
+                def others():
+                    load_exact.start()
+                    for empty in range(1, 4):
+
+                        @pl.when(empty >= count[0])
+                        def clear(empty=empty):
+                            nothing(empty, 0).start()
+                            nothing(empty, 1).start()
+            else:
+
+                @pl.when(k == 0)
+                def second_root():
+                    roots[1].wait()
             halves = []
             for e in (0, 1):
                 block = jnp.concatenate([block_v[k, s, e, 0], block_v[k, s, e, 1]], axis=1)
@@ -678,7 +725,7 @@
     for s in (0, 1):
         rows = pl.ds(s * SEC, SEC)
         own = exact_v[rows, :]
-        wave_v[rows, :] = level[s, 0:1, 0:1] * own + dot(root_v[s], own.astype(BF16))
+        wave_v[rows, :] = level_v[s, 0:1, 0:1] * own + dot(root_v[s], own.astype(BF16))
         waves.append(pltpu.make_async_copy(wave_v.at[rows, :], wave_o.at[rows, :], wave_sem.at[s]))
         waves[s].start()
     for one in waves:
@@ -690,7 +737,6 @@
 
 def renorm(count, source, target, stepped, cols, root, level, exact, energy):
     hbm = pl.BlockSpec(memory_space=pltpu.HBM)
-    vmem = pl.BlockSpec(memory_space=pltpu.VMEM)
     smem = pl.BlockSpec(memory_space=pltpu.SMEM)
     return pl.pallas_call(
         renorm_kernel,
@@ -699,7 +745,7 @@
             jax.ShapeDtypeStruct((2 * SEC, 128), F32),
             jax.ShapeDtypeStruct((1,), F32),
         ),
-        in_specs=[smem] * 3 + [hbm] * 3 + [vmem, hbm, smem],
+        in_specs=[smem] * 3 + [hbm] * 5 + [smem],
         out_specs=(hbm, hbm, smem),
         scratch_shapes=[
             pltpu.VMEM((4, 2, 2, 2, SEC, WIDE), BF16),
@@ -709,12 +755,14 @@
             pltpu.VMEM((SEC, SEC), F32),
             pltpu.VMEM((2 * SEC, 128), F32),
             pltpu.VMEM((2 * SEC, 128), F32),
+            pltpu.VMEM((2, 8, 128), F32),
             pltpu.SemaphoreType.DMA((4, 2, 2)),
             pltpu.SemaphoreType.DMA((4,)),
             pltpu.SemaphoreType.DMA((2,)),
             pltpu.SemaphoreType.DMA((4, 2)),
             pltpu.SemaphoreType.DMA(()),
             pltpu.SemaphoreType.DMA((2,)),
+            pltpu.SemaphoreType.DMA(()),
         ],
         compiler_params=pltpu.CompilerParams(vmem_limit_bytes=60 * MIB),
         name="renorm",

time: 118 us -> 115 us (0.975)
  the two profiles are of different devices: /device:TPU:0 before, /device:TPU:2 now
where the time goes in v4:
time: 115 us
  Pallas kernels  113 us (98%)
  between operations  1.29 us (1%)
    pallas_call x1, Pallas kernels, site(): pl.pallas_call(site_kernel, out_shape=(jax.ShapeDtypeStruct((2, CHIPS, SE...  98.8 us
    pallas_call x1, Pallas kernels, renorm(): pl.pallas_call(renorm_kernel, out_shape=(jax.ShapeDtypeStruct((4, 2 * SEC...  14.6 us

profile of v4, /device:TPU:2, one launch (start us, length us, event | category | flops | bytes accessed | tf_op | source)
XLA Modules:
  0.0 114.7 jit_solution(17239437476118527919)
XLA Ops:
  1.3 98.8 %site.1 = (bf16[2,16,512,256]{3,2,1,0:T(8,128)(2,1)}, bf16[2,512,512]{2,1,0:T(8,128)(2,1)}, f32[2,8,128]{2,1,0:T(8,128)}, f32[1024,128]{1,0:T(8,128)}, f32[8,128]{1,0:T(8,128)}) custom-call(bf16[1024,128]{1,0:T(8,128)(2,1)} %wave.1, bf16[4,1024,512]{2,1,0:T(8,128)(2,1)} %row_ops.1, bf16[4,512,512]{2,1,0:T(8,128)(2,1)} %cols.1, s32[1]{0:T(128)S(6)} %copy.10.count, ...), custom_call_target="tpu_custom_call" | custom-call | tf_op jit(solution)/shard_map/site/pallas_call | solution.py:577
  100.1 14.6 %renorm.1 = (f32[4,1024,512]{2,1,0:T(8,128)}, f32[1024,128]{1,0:T(8,128)}, f32[1]{0:T(128)}) custom-call(s32[1]{0:T(128)S(6)} %copy.10.count, s32[4]{0:T(128)} %source.3, s32[4]{0:T(128)} %target.3, bf16[2,16,512,256]{3,2,1,0:T(8,128)(2,1)} %get-tuple-element.11.stepped, bf16[4,512,512]{2,1,0:T(8,128)(2,1)} %cols.1, ...), custom_call_target="tpu_custom_call" | custom-call | tf_op jit(solution)/shard_map/renorm/pallas_call | solution.py:741

commit v5 on v4

--- a/solution.py
+++ b/solution.py
@@ -335,7 +335,7 @@
     wave, row_ops, col_ops, count, source, target, energy_row,
     stepped_o, root_o, level_o, exact_o, energy_o,
     wide, row_v, col_v, table, table_in, table_s, order_s, source_s, prefix,
-    part, near, whole, near2, whole2, total, summed, stepped, gram, my, mm, mu, mz, roots, level_two, exact, scalars, energy_col,
+    part, near, whole, near2, whole2, total, stepped, gram, my, mm, mu, mz, roots, level_two, exact, scalars, energy_col,
     wv_send, wv_recv, swap_send, swap_recv,
     rs_send, rs_recv, mod_send, mod_recv, rs2_send, rs2_recv, ag_send, ag_recv, en_send, en_recv, st_send, st_recv, st_own,
     end_send, end_recv, own_sem,
@@ -441,21 +441,15 @@
             part[t // 2, 2 * (t % 2) + 1, here, :] = added[:, WIDE:]
         reduction.begin(h)
 
-    for work in (reduction.add, reduction.second, reduction.add2):
-        work(0)
-        work(1)
-    steps = all_blocks(summed, x, z, ag_send, ag_recv, None, CUT, True)
-    for h in (0, 1):
-        reduction.finish(h)
-        here = pl.ds(h * HALF, HALF)
-        summed[b, here, :] = total[here, :].astype(BF16)
-        next(steps)
-    reduction.close()
+    amplitude = wide[b].astype(F32)
+
+    def overlap(i, carry):
+        product = part[lax.div(i, 4), lax.rem(i, 4)].astype(F32) * wide[i].astype(F32)
+        return carry + jnp.sum(product.reshape(SEC // 8, 8, WIDE), axis=0)
+
     level = energy_col[...]
-    amplitude = wide[b].astype(F32)
-    applied = level * amplitude + total[...]
-    share = jnp.sum(amplitude * applied, axis=(0, 1), keepdims=True)
-
+    shares = lax.fori_loop(0, CHIPS, overlap, jnp.sum((level * amplitude * amplitude).reshape(SEC // 8, 8, WIDE), axis=0))
+    share = jnp.sum(shares, axis=(0, 1), keepdims=True)
     stages = (("sec", y, 4), ("x", x, 4), ("z", z, 4), ("core", c, 2))
 
     def energy_copies(s):
@@ -468,14 +462,18 @@
                 push(scalars.at[s, src], scalars.at[s, src], en_send.at[s, hop], en_recv.at[s, hop], to),
             )
 
-    groups = []
+    works = (
+        lambda: (reduction.add(0), reduction.add(1)),
+        lambda: reduction.second(0),
+        lambda: reduction.second(1),
+        lambda: (reduction.add2(0), reduction.add2(1)),
+    )
     for s in range(4):
         place, size = stages[s][1:]
         scalars[s, place] = jnp.broadcast_to(share, (8, 128))
         for out, unused in energy_copies(s):
             out.start()
-        ready = next(steps)
-        groups += [ready] if ready else []
+        works[s]()
         for out, arriving in energy_copies(s):
             arriving.wait_recv()
             out.wait_send()
@@ -485,9 +483,18 @@
         share = share[0:1, 0:1]
     energy = share * (1.0 / ENTRIES)
     energy_o[...] = jnp.broadcast_to(energy, (8, 128))
-    own = amplitude + 0.5 * (energy * amplitude - applied)
-    exact[0] = own[:, :128]
-    exact[1] = own[:, 128:]
+
+    steps = all_blocks(stepped, x, z, ag_send, ag_recv, None, CUT, True)
+    for h in (0, 1):
+        reduction.finish(h)
+        here = pl.ds(h * HALF, HALF)
+        mild = wide[b, here, :].astype(F32)
+        own = mild + 0.5 * (energy * mild - (energy_col[here, :] * mild + total[here, :]))
+        stepped[b, here, :] = own.astype(BF16)
+        next(steps)
+        exact[0, here, :] = own[:, :128]
+        exact[1, here, :] = own[:, 128:]
+    reduction.close()
     exact_send = push(exact.at[1 - c], exact_o.at[mine, :], end_send.at[0], end_recv.at[0], sib)
     exact_own = pltpu.make_async_copy(exact.at[c], exact_o.at[mine, :], own_sem.at[2])
     exact_send.start()
@@ -504,10 +511,7 @@
     def add_group(group):
         def one_block(t, carry):
             i = group_block(group, t, x, z)
-            part_of = wide[i].astype(F32)
-            value = part_of + 0.5 * (energy * part_of - (level * part_of + summed[i].astype(F32)))
-            value = value.astype(BF16)
-            stepped[i] = value
+            value = stepped[i]
             for one in out_block(i):
                 one.start()
             gram[...] += dot_t(value, value)
@@ -515,8 +519,6 @@
 
         lax.fori_loop(0, GROUP_SIZE[group], one_block, 0)
 
-    for group in groups:
-        add_group(group)
     for ready in steps:
         if ready:
             add_group(ready)
@@ -601,7 +603,6 @@
             pltpu.VMEM((2, 2, 2, EIGHTH, WIDE), BF16),
             pltpu.VMEM((2, 2, 2, QUARTER, WIDE), BF16),
             pltpu.VMEM((SEC, WIDE), F32),
-            blocks,
             blocks,
             square,
             square,

time: 115 us -> 110 us (0.957)
  the two profiles are of different devices: /device:TPU:2 before, /device:TPU:1 now
where the time goes in v5:
time: 110 us
  Pallas kernels  109 us (99%)
  between operations  1.29 us (1%)
    pallas_call x1, Pallas kernels, site(): pl.pallas_call(site_kernel, out_shape=(jax.ShapeDtypeStruct((2, CHIPS, SE...  98.4 us
    pallas_call x1, Pallas kernels, renorm(): pl.pallas_call(renorm_kernel, out_shape=(jax.ShapeDtypeStruct((4, 2 * SEC...  10.5 us

profile of v5, /device:TPU:1, one launch (start us, length us, event | category | flops | bytes accessed | tf_op | source)
XLA Modules:
  0.0 110.2 jit_solution(10442681929632009779)
XLA Ops:
  1.3 98.4 %site.1 = (bf16[2,16,512,256]{3,2,1,0:T(8,128)(2,1)}, bf16[2,512,512]{2,1,0:T(8,128)(2,1)}, f32[2,8,128]{2,1,0:T(8,128)}, f32[1024,128]{1,0:T(8,128)}, f32[8,128]{1,0:T(8,128)}) custom-call(bf16[1024,128]{1,0:T(8,128)(2,1)} %wave.1, bf16[4,1024,512]{2,1,0:T(8,128)(2,1)} %row_ops.1, bf16[4,512,512]{2,1,0:T(8,128)(2,1)} %cols.1, s32[1]{0:T(128)S(6)} %copy.10.count, ...), custom_call_target="tpu_custom_call" | custom-call | tf_op jit(solution)/shard_map/site/pallas_call | solution.py:579
  99.7 10.5 %renorm.1 = (f32[4,1024,512]{2,1,0:T(8,128)}, f32[1024,128]{1,0:T(8,128)}, f32[1]{0:T(128)}) custom-call(s32[1]{0:T(128)S(6)} %copy.10.count, s32[4]{0:T(128)} %source.3, s32[4]{0:T(128)} %target.3, bf16[2,16,512,256]{3,2,1,0:T(8,128)(2,1)} %get-tuple-element.11.stepped, bf16[4,512,512]{2,1,0:T(8,128)(2,1)} %cols.1, ...), custom_call_target="tpu_custom_call" | custom-call | tf_op jit(solution)/shard_map/renorm/pallas_call | solution.py:742
